TPU v7x, 256 devices: a whole 4x4x8 slice. The times are simulated.
256 devices in a mesh: seq: 32 (over y_hi, z, core), head: 8 (over x, y_lo).
Axes of the slice: x: 4, y: 4 (y_hi: 2, y_lo: 2; y = y_hi * 2 + y_lo), z: 8, core: 2. Of those that a mesh axis runs over, the one named last changes fastest.
Arguments:
- q_video: bfloat16 [28672, 3072], P('seq', 'head'), may hold values from -160 to 160
- k_video: bfloat16 [8192, 3072], P('seq', 'head'), may hold values from -8 to 8
- video_value_rows: bfloat16 [8192, 3072], P('seq', 'head'), may hold values from -6 to 6
- q_text: bfloat16 [256, 3072], P('seq', 'head'), may hold values from -160 to 160
- k_text: bfloat16 [256, 3072], P('seq', 'head'), may hold values from -8 to 8
- v_text: bfloat16 [256, 3072], P('seq', 'head'), may hold values from -6 to 6
- x_video: bfloat16 [28672, 3072], P('seq', 'head'), may hold values from -24 to 24
- x_text: bfloat16 [256, 3072], P('seq', 'head'), may hold values from -24 to 24
- out_video: bfloat16 [3072, 3072], P('head'), may hold values from -0.109375 to 0.109375
- out_text: bfloat16 [3072, 3072], P('head'), may hold values from -0.109375 to 0.109375
- mod_video: float32 [3, 3072], P(None, 'head'), may hold values from -1.5 to 1.5
- mod_text: float32 [3, 3072], P(None, 'head'), may hold values from -1.5 to 1.5
Outputs:
- x_video_out: bfloat16 [28672, 3072], P('seq', 'head')
- mlp_video_in: bfloat16 [28672, 3072], P('seq', 'head')
- x_text_out: bfloat16 [256, 3072], P('seq', 'head')
- mlp_text_in: bfloat16 [256, 3072], P('seq', 'head')
All inputs are finite; a program needn't handle non-finite values.
Results may differ from a plain program's by a relative error of at most 0.0075.
Values may be sent and summed in bfloat16 or wider, within the bound.
No kernel may reach another device: no remote copies, remote signals or barrier semaphores. Data moves between devices by JAX's collectives and lax.ppermute only.
A program may use at most 128 MiB of HBM per device.

v0:
```python
import functools
import math

import jax
import jax.numpy as jnp
from jax import lax
from jax.experimental import pallas as pl
from jax.experimental.pallas import tpu as pltpu
from jax.sharding import PartitionSpec as P

MODEL_WIDTH = 3072
DH = 128
HERE = 3
WIDTH = HERE * DH
VID = 896
UPPER, LOWER = 480, 416
TXTR = 8
THEIRS = VID + 128
ACC = 144
KB = 256
BLOCK = KB + 16
CHUNKS = MODEL_WIDTH // WIDTH
SUM_ROWS = 1024
SCALE = math.log2(math.e) / math.sqrt(DH)
LIMIT = 1e30
NT = (((1,), (1,)), ((), ()))
F32, BF16 = jnp.float32, jnp.bfloat16
VMEM = pl.BlockSpec(memory_space=pltpu.VMEM)
SMEM = pl.BlockSpec(memory_space=pltpu.SMEM)
ANY = pl.BlockSpec(memory_space=pl.ANY)
HBM = pl.BlockSpec(memory_space=pltpu.HBM)


def params():
    return pltpu.CompilerParams(vmem_limit_bytes=30 * 2**20)


def with_ones(v):
    return jnp.concatenate([v.T, jnp.ones((ACC - DH, v.shape[0]), BF16)], axis=0)


def scores_of(k, q):
    return lax.dot_general(k, q, NT, preferred_element_type=F32) * SCALE


def rows_of(refs, columns):
    return [r[:KB, columns] for r in refs]


def text_of(refs, columns):
    rows = [r[KB:, columns].astype(F32)[:TXTR] for r in refs]
    return jnp.concatenate(rows, axis=0).astype(BF16)


def safe_head(q, keys, values, acc, top):
    for k, v in zip(keys, values, strict=True):
        s = scores_of(k, q)
        new_top = jnp.maximum(top, jnp.max(s, axis=0, keepdims=True))
        p = jnp.exp2(s - new_top).astype(BF16)
        acc = acc * jnp.exp2(top - new_top) + jnp.dot(with_ones(v), p, preferred_element_type=F32)
        top = new_top
    return acc, top


def columns_of(head):
    at = head * DH if isinstance(head, int) else pl.multiple_of(head * DH, DH)
    return pl.ds(at, DH), pl.ds(WIDTH + at, DH)


def attend_kernel(groups, n, texts, first, unread, send, *refs):
    q_refs, refs = refs[:groups], refs[groups:]
    blocks, text_blocks = refs[:n], refs[:texts]
    refs = refs[max(n, texts) + unread :]
    before, after = (None, refs) if first else (refs[: 2 * groups], refs[2 * groups :])

    def text_operands(h):
        key_at, value_at = columns_of(h)
        if not texts:
            return [], []
        return [text_of(text_blocks, key_at)], [text_of(text_blocks, value_at)]

    added, tops = {}, {}
    for h in range(HERE):
        key_at, value_at = columns_of(h)
        keys, values = rows_of(blocks, key_at), rows_of(blocks, value_at)
        pairs = [(keys[i : i + 2], values[i : i + 2]) for i in range(0, n, 2)]
        if texts:
            pairs.append(text_operands(h))
        for g in range(groups):
            q = q_refs[g][:, key_at]
            if first:
                top = jnp.max(scores_of(keys[0][:32], q), axis=0, keepdims=True)
            else:
                top = before[2 * g + 1][h, :1]
            total = None
            for k, v in pairs:
                p = jnp.exp2(scores_of(jnp.concatenate(k, axis=0), q) - top).astype(BF16)
                d = jnp.dot(with_ones(jnp.concatenate(v, axis=0)), p, preferred_element_type=F32)
                total = d if total is None else total + d
            added[g, h], tops[g, h] = total, top
    fine = jnp.max(jnp.concatenate([a[DH : DH + 1] for a in added.values()], axis=1)) < LIMIT

    @pl.when(fine)
    def _():
        for (g, h), total in added.items():
            after[2 * g][h] = total if first else before[2 * g][h] + total
            after[2 * g + 1][h] = jnp.broadcast_to(tops[g, h], (8, total.shape[1]))

    @pl.when(jnp.logical_not(fine))
    def _():
        @pl.loop(0, HERE)
        def _(h):
            key_at, value_at = columns_of(h)
            for g in range(groups):

                @pl.loop(0, q_refs[g].shape[0] // 128)
                def _(i):
                    lanes = pl.ds(pl.multiple_of(i * 128, 128), 128)
                    more_keys, more_values = text_operands(h)
                    if first:
                        acc, top = jnp.zeros((ACC, 128), F32), jnp.full((1, 128), -1e30, F32)
                    else:
                        acc, top = before[2 * g][h, :, lanes], before[2 * g + 1][h, :1, lanes]
                    acc, top = safe_head(
                        q_refs[g][lanes, key_at],
                        rows_of(blocks, key_at) + more_keys,
                        rows_of(blocks, value_at) + more_values,
                        acc,
                        top,
                    )
                    after[2 * g][h, :, lanes] = acc
                    after[2 * g + 1][h, :, lanes] = jnp.broadcast_to(top, (8, 128))

    if send:
        acc_ref, top_ref, sent_ref = after
        row = lax.broadcasted_iota(jnp.int32, (ACC - DH, acc_ref.shape[2]), 0)

        @pl.loop(0, HERE)
        def _(h):
            total = acc_ref[h, DH : DH + 1]
            inverse = 1.0 / total
            level = top_ref[h, :1] + jnp.log2(total)
            hi = level.astype(BF16).astype(F32)
            mid = (level - hi).astype(BF16).astype(F32)
            low = level - hi - mid
            levels = jnp.where(row == 0, hi, jnp.where(row == 1, mid, jnp.where(row == 2, low, 0.0)))
            sent_ref[h, :DH] = (acc_ref[h, :DH] * inverse).astype(BF16)
            sent_ref[h, DH:] = levels.astype(BF16)


def attend(queries, blocks, states=None, every=(), unread=(), send=False):
    n, texts, groups = len(blocks), len(every), len(queries)
    blocks = [*blocks, *[b for b in every if all(b is not c for c in blocks)]]
    keys = n * KB + texts * TXTR
    lanes = sum(q.shape[0] for q in queries)
    out_shape = []
    for q in queries:
        out_shape.append(jax.ShapeDtypeStruct((HERE, ACC, q.shape[0]), F32))
        out_shape.append(jax.ShapeDtypeStruct((HERE, 8, q.shape[0]), F32))
    if send:
        out_shape.append(jax.ShapeDtypeStruct((HERE, ACC, queries[0].shape[0]), BF16))
    first = states is None
    states = [] if first else states
    before = groups + len(blocks) + len(unread)
    return pl.pallas_call(
        functools.partial(attend_kernel, groups, n, texts, first, len(unread), send),
        in_specs=[VMEM] * (groups + len(blocks)) + [ANY] * len(unread) + [VMEM] * len(states),
        out_specs=[VMEM] * len(out_shape),
        out_shape=out_shape,
        input_output_aliases={before + i: i for i in range(len(states))},
        compiler_params=params(),
        cost_estimate=pl.CostEstimate(
            flops=HERE * lanes * keys * DH * 8,
            bytes_accessed=HERE * ACC * lanes * 4,
            transcendentals=HERE * lanes * keys,
        ),
        name="attend",
    )(*queries, *blocks, *unread, *states)


def merged(acc, top, got):
    total = acc[DH : DH + 1]
    mine = top + jnp.log2(total)
    theirs = got[DH : DH + 1] + got[DH + 1 : DH + 2] + got[DH + 2 : DH + 3]
    share = 1.0 / (1.0 + jnp.exp2(theirs - mine))
    other = 1.0 / (1.0 + jnp.exp2(mine - theirs))
    return acc[:DH] * (share / total) + got[:DH] * other


def combine_kernel(
    acc_ref, top_ref, text_acc, text_top, got_ref, w_hbm, upper_ref, lower_ref, w_ref, rows_ref, sem
):
    copy = pltpu.make_async_copy(w_hbm, w_ref, sem)
    copy.start()

    @pl.loop(0, HERE)
    def _(h):
        at, _ = columns_of(h)
        video = merged(acc_ref[h], top_ref[h, :1], got_ref[h, :, :VID].astype(F32)).T.astype(BF16)
        upper_ref[:, at] = video[:UPPER]
        lower_ref[:LOWER, at] = video[UPPER:]
        got = pltpu.roll(got_ref[h, :, VID:].astype(F32), DH - TXTR, 1)
        rows = merged(text_acc[h, :, VID:], text_top[h, :1, VID:], got).T
        rows_ref[:, at] = rows[: 2 * TXTR].astype(BF16)

    copy.wait()
    part = jnp.dot(rows_ref[...], w_ref[...], preferred_element_type=F32)[:TXTR]
    chunks = [part[:, j * WIDTH : (j + 1) * WIDTH] for j in range(CHUNKS)]
    lower_ref[LOWER:] = jnp.concatenate(chunks, axis=0).astype(BF16)


def combine(own, theirs, got, out_text):
    return pl.pallas_call(
        combine_kernel,
        in_specs=[VMEM] * 5 + [HBM],
        out_specs=[VMEM] * 2,
        out_shape=[
            jax.ShapeDtypeStruct((UPPER, WIDTH), BF16),
            jax.ShapeDtypeStruct((LOWER + CHUNKS * TXTR, WIDTH), BF16),
        ],
        scratch_shapes=[
            pltpu.VMEM((WIDTH, MODEL_WIDTH), BF16),
            pltpu.VMEM((2 * TXTR, WIDTH), BF16),
            pltpu.SemaphoreType.DMA(()),
        ],
        compiler_params=params(),
        cost_estimate=pl.CostEstimate(flops=10**9, bytes_accessed=10**7, transcendentals=0),
        name="combine",
    )(*own, *theirs, got, out_text)


def slice_kernel(steps, unread, at_ref, w_ref, *refs):
    out_refs, sems = refs[unread : unread + len(steps)], refs[unread + len(steps) :]
    copies = []
    for k, out_ref, sem in zip(steps, out_refs, sems, strict=True):
        first = lax.rem(at_ref[0] + 4 - k, 4) * (2 * WIDTH)
        columns = pl.ds(pl.multiple_of(first, 2 * WIDTH), 2 * WIDTH)
        copies.append(pltpu.make_async_copy(w_ref.at[:, columns], out_ref, sem))
        copies[-1].start()
    for copy in copies:
        copy.wait()


def column_slices(at, weight, steps, unread=()):
    return pl.pallas_call(
        functools.partial(slice_kernel, steps, len(unread)),
        in_specs=[SMEM, HBM] + [ANY] * len(unread),
        out_specs=[VMEM] * len(steps),
        out_shape=[jax.ShapeDtypeStruct((WIDTH, 2 * WIDTH), BF16)] * len(steps),
        scratch_shapes=[pltpu.SemaphoreType.DMA(())] * len(steps),
        compiler_params=params(),
        name="columns",
    )(at, weight, *unread)


def own_kernel(arrived_ref, upper_ref, lower_ref, w_ref, upper_out, lower_out, again_ref):
    del arrived_ref
    again_ref[...] = lower_ref[...]
    upper_out[...] = jnp.dot(upper_ref[...], w_ref[...], preferred_element_type=F32)
    lower_out[...] = jnp.dot(lower_ref[:LOWER], w_ref[...], preferred_element_type=F32)


def project_own(arrived, upper, lower, weight):
    return pl.pallas_call(
        own_kernel,
        in_specs=[ANY] + [VMEM] * 3,
        out_specs=[VMEM] * 3,
        out_shape=[
            *[jax.ShapeDtypeStruct((rows, 2 * WIDTH), F32) for rows in (UPPER, LOWER)],
            jax.ShapeDtypeStruct(lower.shape, BF16),
        ],
        compiler_params=params(),
        cost_estimate=pl.CostEstimate(flops=10**9, bytes_accessed=5 * 10**6, transcendentals=0),
        name="project_own",
    )(arrived, upper, lower, weight)


def more_kernel(sum_ref, one_ref, two_ref, w_one, w_two, out_ref):
    rows = sum_ref.shape[0]
    out_ref[...] = (
        sum_ref[...]
        + jnp.dot(one_ref[:rows], w_one[...], preferred_element_type=F32)
        + jnp.dot(two_ref[:rows], w_two[...], preferred_element_type=F32)
    )


def project_more(total, one, two, w_one, w_two):
    return pl.pallas_call(
        more_kernel,
        in_specs=[VMEM] * 5,
        out_specs=VMEM,
        out_shape=jax.ShapeDtypeStruct(total.shape, F32),
        input_output_aliases={0: 0},
        compiler_params=params(),
        cost_estimate=pl.CostEstimate(flops=10**9, bytes_accessed=5 * 10**6, transcendentals=0),
        name="project_more",
    )(total, one, two, w_one, w_two)


def last_kernel(at_ref, sum_ref, *refs):
    att, w_ref, sent_ref, mine_ref = refs[:-3], refs[-3], refs[-2], refs[-1]
    left = at_ref[1] == 0
    count = sum_ref.shape[0]
    rows = sum_ref[...] + jnp.dot(att[0][:count], w_ref[...], preferred_element_type=F32)
    one, two = rows[:, :WIDTH], rows[:, WIDTH:]
    mine_ref[:count] = jnp.where(left, one, two)
    sent_ref[:count] = jnp.where(left, two, one).astype(BF16)
    if len(att) > 1:
        at = pl.ds(pl.multiple_of(count + at_ref[0] * (2 * TXTR), 2 * TXTR), 2 * TXTR)
        text = sum(a[at].astype(F32) for a in att)
        mine = jnp.where(left, text[:TXTR], text[TXTR:])
        sent = jnp.where(left, text[TXTR:], text[:TXTR])
        mine_ref[count:] = jnp.concatenate([mine, mine], axis=0)
        sent_ref[count:] = jnp.concatenate([sent, sent], axis=0).astype(BF16)


def project_last(at, total, att, weight):
    rows = total.shape[0] + (2 * TXTR if len(att) > 1 else 0)
    return pl.pallas_call(
        last_kernel,
        in_specs=[SMEM] + [VMEM] * (2 + len(att)),
        out_specs=[VMEM] * 2,
        out_shape=[jax.ShapeDtypeStruct((rows, WIDTH), BF16), jax.ShapeDtypeStruct((rows, WIDTH), F32)],
        compiler_params=params(),
        cost_estimate=pl.CostEstimate(flops=10**9, bytes_accessed=5 * 10**6, transcendentals=0),
        name="project_last",
    )(at, total, *att, weight)


def residual_kernel(
    own_a, got_a, own_b, got_b, xv_ref, xt_ref, mv_ref, mt_ref, xv_out, xt_out, res_ref, sums_ref
):
    gate = mv_ref[:1]
    upper = xv_ref[:UPPER].astype(F32) + gate * (own_a[...] + got_a[...].astype(F32))
    lower = xv_ref[UPPER:].astype(F32) + gate * (own_b[:LOWER] + got_b[:LOWER].astype(F32))
    text_proj = own_b[LOWER:] + got_b[LOWER:].astype(F32)
    text = xt_ref[...].astype(F32) + mt_ref[:1] * text_proj[:TXTR]
    xv_out[:UPPER] = upper.astype(BF16)
    xv_out[UPPER:] = lower.astype(BF16)
    xt_out[...] = text.astype(BF16)
    rows = jnp.concatenate([upper, lower, text], axis=0)
    res_ref[...] = rows
    count = VID + TXTR
    lane = lax.broadcasted_iota(jnp.int32, (count, 128), 1)
    sums = jnp.where(
        lane == 0,
        jnp.sum(rows, axis=1, keepdims=True),
        jnp.where(lane == 1, jnp.sum(rows * rows, axis=1, keepdims=True), 0.0),
    )
    sums = jnp.concatenate([sums, jnp.zeros((SUM_ROWS - count, 128), F32)], axis=0)
    sums_ref[...] = sums.T[:8]


def norm_kernel(res_ref, mv_ref, mt_ref, s0_ref, s1_ref, s2_ref, s3_ref, video_out, text_out):
    sums = (s0_ref[...] + s1_ref[...]) + (s2_ref[...] + s3_ref[...])
    sums = jnp.concatenate([sums, jnp.zeros((120, SUM_ROWS), F32)], axis=0).T
    mean = sums[: VID + TXTR, :1] / MODEL_WIDTH
    var = sums[: VID + TXTR, 1:2] / MODEL_WIDTH - mean * mean
    normed = (res_ref[...] - mean) * lax.rsqrt(var + 1e-06)
    video_out[...] = (normed[:VID] * (1.0 + mv_ref[2:3]) + mv_ref[1:2]).astype(BF16)
    text_out[...] = (normed[VID:] * (1.0 + mt_ref[2:3]) + mt_ref[1:2]).astype(BF16)


def local(
    q_video, k_video, video_value_rows, q_text, k_text, v_text, x_video, x_text, out_video, out_text, mod_video, mod_text
):
    def over_seq(move):
        pairs = []
        for y in range(2):
            for z in range(8):
                for c in range(2):
                    a, b, d = move(y, z, c)
                    pairs.append(((y * 8 + z) * 2 + c, ((a % 2) * 8 + b % 8) * 2 + d % 2))
        return lambda value: lax.ppermute(value, "seq", pairs)

    def over_head(move):
        pairs = []
        for x in range(4):
            for y in range(2):
                a, b = move(x, y)
                pairs.append((x * 2 + y, (a % 4) * 2 + b % 2))
        return lambda value: lax.ppermute(value, "head", pairs)

    other_core = over_seq(lambda y, z, c: (y, z, 1 - c))
    other_plane = over_seq(lambda y, z, c: (1 - y, z, c))
    up = over_seq(lambda y, z, c: (y, z + 1, c))
    down = over_seq(lambda y, z, c: (y, z - 1, c))
    across = over_seq(lambda y, z, c: (1 - y, z - 1, c))
    from_on = [None] + [over_head(lambda x, y, k=k: (x - k, y)) for k in (1, 2, 3)]
    pair = over_head(lambda x, y: (x, 1 - y))

    head = lax.axis_index("head")
    x_at = head // 2
    at = jnp.stack([x_at, head % 2]).astype(jnp.int32)

    own = jnp.concatenate(
        [
            jnp.concatenate([k_video, video_value_rows], axis=1),
            jnp.concatenate([k_text, v_text], axis=1),
            jnp.zeros((BLOCK - KB - TXTR, 2 * WIDTH), BF16),
        ],
        axis=0,
    )
    q_other = other_core(jnp.concatenate([q_video, q_text], axis=0))
    y0, r1, l1 = other_plane(own), up(own), down(own)
    r2, l2 = up(r1), down(l1)
    yr1, yl1 = other_plane(r1), other_plane(l1)
    r3, l3 = up(r2), down(l2)
    ry2, ly2 = up(yr1), down(yl1)
    r4, opposite = up(r3), across(l3)
    ry3, ly3 = up(ry2), down(ly2)

    slice_1 = lax.dynamic_slice_in_dim(out_video, lax.rem(x_at + 3, 4) * 2 * WIDTH, 2 * WIDTH, axis=1)
    weight_1 = from_on[1](slice_1)
    here, slice_2 = column_slices(at, out_video, (0, 2), unread=[weight_1])
    weight_2 = from_on[2](slice_2)
    [slice_3] = column_slices(at, out_video, (3,), unread=[weight_2])
    weights = [here, weight_1, weight_2, from_on[3](slice_3)]

    q_theirs = jnp.concatenate(
        [q_other[:VID], q_text, q_other[VID:], jnp.zeros((THEIRS - VID - 2 * TXTR, WIDTH), BF16)], axis=0
    )
    queries = [q_theirs, q_video]
    states = attend(queries, [own, r1, l1, y0])
    states = attend(queries, [r2, l2, yr1, yl1], states, unread=weights[1:2])
    states = attend(queries, [r3, l3, ry2, ly2], states, unread=weights[2:3])
    states = attend(queries, [r4, opposite], states)
    every = [ry3, ly3, own, r1, l1, y0, r2, l2, yr1, yl1, r3, l3, ry2, ly2, r4, opposite]
    *theirs, sent = attend(queries[:1], [ry3, ly3], states[:2], every=every, unread=weights[3:], send=True)
    got = other_core(sent)
    mine = attend(queries[1:], [ry3, ly3], states[2:], every=every)

    upper, lower = combine(mine, theirs, got, out_text)
    upper_1, upper_3, lower_3 = from_on[1](upper), from_on[3](upper), from_on[3](lower)
    upper_2 = from_on[1](upper_1)
    sum_a, sum_b, lower_again = project_own(upper_1, upper, lower, weights[0])
    lower_1, lower_2 = from_on[1](lower_again), from_on[3](lower_3)
    sum_a = project_more(sum_a, upper_1, upper_3, weights[1], weights[3])
    sent_a, own_a = project_last(at, sum_a, [upper_2], weights[2])
    got_a = pair(sent_a)
    sum_b = project_more(sum_b, lower_1, lower_3, weights[1], weights[3])
    sent_b, own_b = project_last(at, sum_b, [lower_2, lower, lower_1, lower_3], weights[2])
    got_b = pair(sent_b)

    x_video_out, x_text_out, residual, sums = pl.pallas_call(
        residual_kernel,
        in_specs=[VMEM] * 8,
        out_specs=[VMEM] * 4,
        out_shape=[
            jax.ShapeDtypeStruct((VID, WIDTH), BF16),
            jax.ShapeDtypeStruct((TXTR, WIDTH), BF16),
            jax.ShapeDtypeStruct((VID + TXTR, WIDTH), F32),
            jax.ShapeDtypeStruct((8, SUM_ROWS), F32),
        ],
        compiler_params=params(),
        name="residual",
    )(own_a, got_a, own_b, got_b, x_video, x_text, mod_video, mod_text)
    sums = sums + pair(sums)
    mlp_video_in, mlp_text_in = pl.pallas_call(
        norm_kernel,
        in_specs=[VMEM] * 7,
        out_specs=[VMEM] * 2,
        out_shape=[jax.ShapeDtypeStruct((VID, WIDTH), BF16), jax.ShapeDtypeStruct((TXTR, WIDTH), BF16)],
        compiler_params=params(),
        name="norm",
    )(residual, mod_video, mod_text, sums, *[from_on[k](sums) for k in (1, 2, 3)])
    return x_video_out, mlp_video_in, x_text_out, mlp_text_in


def solution(mesh):
    tokens, rows, columns = P("seq", "head"), P("head", None), P(None, "head")
    return jax.shard_map(
        local,
        mesh=mesh,
        in_specs=(tokens,) * 8 + (rows, rows, columns, columns),
        out_specs=(tokens,) * 4,
        check_vma=False,
    )
```

profile of v0, /device:TPU:8, one launch (start us, length us, event | category | flops | bytes accessed | tf_op | source)
XLA Modules:
  0.0 288.2 jit_solution(8212676167762670269)
XLA Ops:
  4.8 2.8 collective-permute-start.16
  8.8 5.9 %collective-permute-start.4 = (bf16[272,768]{1,0:T(8,128)(2,1)S(1)}, bf16[272,768]{1,0:T(8,128)(2,1)}, u32[]{:S(2)}, u32[]{:S(2)}) collective-permute-start(bf16[272,768]{1,0:T(8,128)(2,1)S(1)} %maximum_maximum_fusion.1.refs_2_.refs_3_), channel_id=1, source_target_pairs={{0,112},{8,120},{16,0},{24,8},{32,16},{40,24},{48,32},{56,40},{64,... | collective-permute-start | bytes 1253384 | tf_op jit(solution)/shard_map/ppermute | solution.py:374
  17.2 6.8 %collective-permute-done.4.refs_4_.refs_5_ = bf16[272,768]{1,0:T(8,128)(2,1)} collective-permute-done((bf16[272,768]{1,0:T(8,128)(2,1)S(1)}, bf16[272,768]{1,0:T(8,128)(2,1)}, u32[]{:S(2)}, u32[]{:S(2)}) %collective-permute-start.4) | collective-permute-done | bytes 417824 | tf_op jit(solution)/shard_map/ppermute | solution.py:374
  24.0 3.8 %collective-permute-start.10 = (bf16[272,768]{1,0:T(8,128)(2,1)}, bf16[272,768]{1,0:T(8,128)(2,1)S(1)}, u32[]{:S(2)}, u32[]{:S(2)}) collective-permute-start(bf16[272,768]{1,0:T(8,128)(2,1)} %collective-permute-done.4.refs_4_.refs_5_), channel_id=1, source_target_pairs={{0,112},{8,120},{16,0},{24,8},{32,16},{40,24},{48,32},{56,40},{64,... | collective-permute-start | bytes 1253384 | tf_op jit(solution)/shard_map/ppermute | solution.py:374
  27.8 2.3 collective-permute-start.5
  35.4 37.9 %attend.6 = (f32[3,144,1024]{2,1,0:T(8,128)S(1)}, f32[3,8,1024]{2,1,0:T(8,128)S(1)}, f32[3,144,896]{2,1,0:T(8,128)S(1)}, f32[3,8,896]{2,1,0:T(8,128)S(1)}) custom-call(bf16[1024,384]{1,0:T(8,128)(2,1)S(1)} %maximum_maximum_fusion.refs_0_, bf16[896,384]{1,0:T(8,128)(2,1)S(1)} %copy-done.1, bf16[272,768]{1,0:T(8,128)(2,1)S(1)} %maximum_maximum_fusion.1.refs_2_.refs_3_, ...), custom_call_target="tpu_custom_call" | custom-call | flops 6039797760 | bytes 3317760 | tf_op jit(solution)/shard_map/attend/pallas_call | solution.py:165
  73.4 3.2 %collective-permute-start.12 = (bf16[272,768]{1,0:T(8,128)(2,1)S(1)}, bf16[272,768]{1,0:T(8,128)(2,1)S(1)}, u32[]{:S(2)}, u32[]{:S(2)}) collective-permute-start(bf16[272,768]{1,0:T(8,128)(2,1)S(1)} %collective-permute-done.10.refs_3_.refs_8_), channel_id=1, source_target_pairs={{0,112},{8,120},{16,0},{24,8},{32,16},{40,24},{48,32},{56,40},{64,... | collective-permute-start | bytes 1253384 | tf_op jit(solution)/shard_map/ppermute | solution.py:374
  76.7 3.6 %collective-permute-start.6 = (bf16[272,768]{1,0:T(8,128)(2,1)S(1)}, bf16[272,768]{1,0:T(8,128)(2,1)S(1)}, u32[]{:S(2)}, u32[]{:S(2)}) collective-permute-start(bf16[272,768]{1,0:T(8,128)(2,1)S(1)} %collective-permute-done.5.refs_5_.refs_10_), channel_id=1, source_target_pairs={{0,112},{8,120},{16,0},{24,8},{32,16},{40,24},{48,32},{56,40},{64,... | collective-permute-start | bytes 1253384 | tf_op jit(solution)/shard_map/ppermute | solution.py:374
  80.3 36.0 %attend.7 = (f32[3,144,1024]{2,1,0:T(8,128)S(1)}, f32[3,8,1024]{2,1,0:T(8,128)S(1)}, f32[3,144,896]{2,1,0:T(8,128)S(1)}, f32[3,8,896]{2,1,0:T(8,128)S(1)}) custom-call(bf16[1024,384]{1,0:T(8,128)(2,1)S(1)} %maximum_maximum_fusion.refs_0_, bf16[896,384]{1,0:T(8,128)(2,1)S(1)} %copy-done.1, ...), custom_call_target="tpu_custom_call", output_to_operand_aliasing={{0}: (7, {}), {1}: (8, {}), {2}: (9, {}), {3}: (10, {})} | custom-call | flops 6039797760 | bytes 3317760 | tf_op jit(solution)/shard_map/attend/pallas_call | solution.py:165
  117.9 5.0 %collective-permute-start.14 = (bf16[272,768]{1,0:T(8,128)(2,1)S(1)}, bf16[272,768]{1,0:T(8,128)(2,1)S(1)}, u32[]{:S(2)}, u32[]{:S(2)}) collective-permute-start(bf16[272,768]{1,0:T(8,128)(2,1)S(1)} %collective-permute-done.12.refs_3_.refs_12_), channel_id=1, source_target_pairs={{0,240},{8,248},{16,128},{24,136},{32,144},{40,152},{48,160},{56,1... | collective-permute-start | bytes 1253384 | tf_op jit(solution)/shard_map/ppermute | solution.py:374
  122.9 3.4 %collective-permute-start.7 = (bf16[272,768]{1,0:T(8,128)(2,1)S(1)}, bf16[272,768]{1,0:T(8,128)(2,1)S(1)}, u32[]{:S(2)}, u32[]{:S(2)}) collective-permute-start(bf16[272,768]{1,0:T(8,128)(2,1)S(1)} %collective-permute-done.6.refs_5_.refs_14_), channel_id=1, source_target_pairs={{0,112},{8,120},{16,0},{24,8},{32,16},{40,24},{48,32},{56,40},{64,... | collective-permute-start | bytes 1253384 | tf_op jit(solution)/shard_map/ppermute | solution.py:374
  126.3 36.0 %attend.8 = (f32[3,144,1024]{2,1,0:T(8,128)S(1)}, f32[3,8,1024]{2,1,0:T(8,128)S(1)}, f32[3,144,896]{2,1,0:T(8,128)S(1)}, f32[3,8,896]{2,1,0:T(8,128)S(1)}) custom-call(bf16[1024,384]{1,0:T(8,128)(2,1)S(1)} %maximum_maximum_fusion.refs_0_, bf16[896,384]{1,0:T(8,128)(2,1)S(1)} %copy-done.1, ...), custom_call_target="tpu_custom_call", output_to_operand_aliasing={{0}: (7, {}), {1}: (8, {}), {2}: (9, {}), {3}: (10, {})} | custom-call | flops 6039797760 | bytes 3317760 | tf_op jit(solution)/shard_map/attend/pallas_call | solution.py:165
  162.3 30.7 %attend.9 = (f32[3,144,1024]{2,1,0:T(8,128)S(1)}, f32[3,8,1024]{2,1,0:T(8,128)S(1)}, f32[3,144,896]{2,1,0:T(8,128)S(1)}, f32[3,8,896]{2,1,0:T(8,128)S(1)}) custom-call(bf16[1024,384]{1,0:T(8,128)(2,1)S(1)} %maximum_maximum_fusion.refs_0_, bf16[896,384]{1,0:T(8,128)(2,1)S(1)} %copy-done.1, ...), custom_call_target="tpu_custom_call", output_to_operand_aliasing={{0}: (4, {}), {1}: (5, {}), {2}: (6, {}), {3}: (7, {})} | custom-call | flops 3019898880 | bytes 3317760 | tf_op jit(solution)/shard_map/attend/pallas_call | solution.py:165
  193.1 19.3 %attend.11 = (f32[3,144,1024]{2,1,0:T(8,128)S(1)}, f32[3,8,1024]{2,1,0:T(8,128)S(1)}, bf16[3,144,1024]{2,1,0:T(8,128)(2,1)S(1)}) custom-call(bf16[1024,384]{1,0:T(8,128)(2,1)S(1)} %maximum_maximum_fusion.refs_0_, bf16[272,768]{1,0:T(8,128)(2,1)S(1)} %collective-permute-done.3.refs_1_, ...), custom_call_target="tpu_custom_call", output_to_operand_aliasing={{0}: (18, {}), {1}: (19, {})} | custom-call | flops 2013265920 | bytes 1769472 | tf_op jit(solution)/shard_map/attend/pallas_call | solution.py:165
  212.5 17.1 %attend.10 = (f32[3,144,896]{2,1,0:T(8,128)S(1)}, f32[3,8,896]{2,1,0:T(8,128)S(1)}) custom-call(bf16[896,384]{1,0:T(8,128)(2,1)S(1)} %copy-done.1, bf16[272,768]{1,0:T(8,128)(2,1)S(1)} %collective-permute-done.3.refs_1_, bf16[272,768]{1,0:T(8,128)(2,1)S(1)} %collective-permute-done.7.refs_2_, ...), custom_call_target="tpu_custom_call", output_to_operand_aliasing={{0}: (17, {}), {1}: (18, {})} | custom-call | flops 1761607680 | bytes 1548288 | tf_op jit(solution)/shard_map/attend/pallas_call | solution.py:165
  230.9 2.4 collective-permute-start.20
  234.8 7.2 %collective-permute-done.20.arrived_ref.one_ref = bf16[480,384]{1,0:T(8,128)(2,1)S(1)} collective-permute-done((bf16[480,384]{1,0:T(8,128)(2,1)S(1)}, bf16[480,384]{1,0:T(8,128)(2,1)S(1)}, u32[]{:S(2)}, u32[]{:S(2)}) %collective-permute-start.20) | collective-permute-done | bytes 368672 | tf_op jit(solution)/shard_map/ppermute | solution.py:382
  242.0 3.5 %collective-permute-start.22 = (bf16[480,384]{1,0:T(8,128)(2,1)S(1)}, bf16[480,384]{1,0:T(8,128)(2,1)S(1)}, u32[]{:S(2)}, u32[]{:S(2)}) collective-permute-start(bf16[480,384]{1,0:T(8,128)(2,1)S(1)} %collective-permute-done.20.arrived_ref.one_ref), channel_id=1, source_target_pairs={{0,6},{1,7},{2,0},{3,1},{4,2},{5,3},{6,4},{7,5},{8,14},{9,15},{10,... | collective-permute-start | bytes 1105928 | tf_op jit(solution)/shard_map/ppermute | solution.py:382
  248.7 5.1 %collective-permute-done.21.two_ref = bf16[480,384]{1,0:T(8,128)(2,1)S(1)} collective-permute-done((bf16[480,384]{1,0:T(8,128)(2,1)S(1)}, bf16[480,384]{1,0:T(8,128)(2,1)S(1)}, u32[]{:S(2)}, u32[]{:S(2)}) %collective-permute-start.21) | collective-permute-done | bytes 368672 | tf_op jit(solution)/shard_map/ppermute | solution.py:382
  257.6 3.5 %collective-permute-done.24.one_ref.refs_2_ = bf16[480,384]{1,0:T(8,128)(2,1)S(1)} collective-permute-done((bf16[480,384]{1,0:T(8,128)(2,1)S(1)}, bf16[480,384]{1,0:T(8,128)(2,1)S(1)}, u32[]{:S(2)}, u32[]{:S(2)}) %collective-permute-start.24) | collective-permute-done | bytes 368672 | tf_op jit(solution)/shard_map/ppermute | solution.py:382
  264.7 7.8 %collective-permute-done.27.got_b = bf16[432,384]{1,0:T(8,128)(2,1)S(1)} collective-permute-done((bf16[432,384]{1,0:T(8,128)(2,1)S(1)}, bf16[432,384]{1,0:T(8,128)(2,1)S(1)}, u32[]{:S(2)}, u32[]{:S(2)}) %collective-permute-start.27) | collective-permute-done | bytes 331808 | tf_op jit(solution)/shard_map/ppermute | solution.py:382
  275.1 2.6 collective-permute-done.28
  277.6 3.1 %collective-permute-start.29 = (f32[8,1024]{1,0:T(8,128)S(1)}, f32[8,1024]{1,0:T(8,128)S(1)}, u32[]{:S(2)}, u32[]{:S(2)}) collective-permute-start(f32[8,1024]{1,0:T(8,128)S(1)} %add.17.s0_ref), channel_id=1, source_target_pairs={{0,6},{1,7},{2,0},{3,1},{4,2},{5,3},{6,4},{7,5},{8,14},{9,15},{10,... | collective-permute-start | bytes 98312 | tf_op jit(solution)/shard_map/ppermute | solution.py:382
  282.3 3.9 %collective-permute-done.30.s2_ref = f32[8,1024]{1,0:T(8,128)S(1)} collective-permute-done((f32[8,1024]{1,0:T(8,128)S(1)}, f32[8,1024]{1,0:T(8,128)S(1)}, u32[]{:S(2)}, u32[]{:S(2)}) %collective-permute-start.30) | collective-permute-done | bytes 32800 | tf_op jit(solution)/shard_map/ppermute | solution.py:382
  (88 shorter events, 33.8 us)
Async XLA Ops:
  2.9 29.2 %collective-permute-start.15 = (bf16[904,384]{1,0:T(8,128)(2,1)}, bf16[904,384]{1,0:T(8,128)(2,1)}, u32[]{:S(2)}, u32[]{:S(2)}) collective-permute-start(bf16[904,384]{1,0:T(8,128)(2,1)} %pad_maximum_fusion), channel_id=1, source_target_pairs={{0,8},{8,0},{16,24},{24,16},{32,40},{40,32},{48,56},{56,48},{64,72... | collective-permute-start | bytes 2082824 | tf_op jit(solution)/shard_map/ppermute | solution.py:374
  4.8 25.3 %collective-permute-start.16 = (bf16[384,768]{1,0:T(8,128)(2,1)}, bf16[384,768]{1,0:T(8,128)(2,1)S(1)}, u32[]{:S(2)}, u32[]{:S(2)}) collective-permute-start(bf16[384,768]{1,0:T(8,128)(2,1)} %constant_dynamic-slice_fusion), channel_id=1, source_target_pairs={{0,6},{1,7},{2,0},{3,1},{4,2},{5,3},{6,4},{7,5},{8,14},{9,15},{10,... | collective-permute-start | bytes 1769480 | tf_op jit(solution)/shard_map/ppermute | solution.py:382
  8.8 15.2 %collective-permute-start.4 = (bf16[272,768]{1,0:T(8,128)(2,1)S(1)}, bf16[272,768]{1,0:T(8,128)(2,1)}, u32[]{:S(2)}, u32[]{:S(2)}) collective-permute-start(bf16[272,768]{1,0:T(8,128)(2,1)S(1)} %maximum_maximum_fusion.1.refs_2_.refs_3_), channel_id=1, source_target_pairs={{0,112},{8,120},{16,0},{24,8},{32,16},{40,24},{48,32},{56,40},{64,... | collective-permute-start | bytes 1253384 | tf_op jit(solution)/shard_map/ppermute | solution.py:374
  14.7 19.6 %collective-permute-start.8 = (bf16[272,768]{1,0:T(8,128)(2,1)S(1)}, bf16[272,768]{1,0:T(8,128)(2,1)}, u32[]{:S(2)}, u32[]{:S(2)}) collective-permute-start(bf16[272,768]{1,0:T(8,128)(2,1)S(1)} %maximum_maximum_fusion.1.refs_2_.refs_3_), channel_id=1, source_target_pairs={{0,128},{8,136},{16,144},{24,152},{32,160},{40,168},{48,176},{56,1... | collective-permute-start | bytes 1253384 | tf_op jit(solution)/shard_map/ppermute | solution.py:374
  24.0 49.4 %collective-permute-start.10 = (bf16[272,768]{1,0:T(8,128)(2,1)}, bf16[272,768]{1,0:T(8,128)(2,1)S(1)}, u32[]{:S(2)}, u32[]{:S(2)}) collective-permute-start(bf16[272,768]{1,0:T(8,128)(2,1)} %collective-permute-done.4.refs_4_.refs_5_), channel_id=1, source_target_pairs={{0,112},{8,120},{16,0},{24,8},{32,16},{40,24},{48,32},{56,40},{64,... | collective-permute-start | bytes 1253384 | tf_op jit(solution)/shard_map/ppermute | solution.py:374
  27.8 48.9 %collective-permute-start.5 = (bf16[272,768]{1,0:T(8,128)(2,1)}, bf16[272,768]{1,0:T(8,128)(2,1)S(1)}, u32[]{:S(2)}, u32[]{:S(2)}) collective-permute-start(bf16[272,768]{1,0:T(8,128)(2,1)} %collective-permute-done.4.refs_4_.refs_5_), channel_id=1, source_target_pairs={{0,128},{8,136},{16,144},{24,152},{32,160},{40,168},{48,176},{56,1... | collective-permute-start | bytes 1253384 | tf_op jit(solution)/shard_map/ppermute | solution.py:374
  30.1 46.5 %collective-permute-start.1 = (bf16[272,768]{1,0:T(8,128)(2,1)}, bf16[272,768]{1,0:T(8,128)(2,1)S(1)}, u32[]{:S(2)}, u32[]{:S(2)}) collective-permute-start(bf16[272,768]{1,0:T(8,128)(2,1)} %collective-permute-done.refs_3_.refs_4_), channel_id=1, source_target_pairs={{0,128},{8,136},{16,144},{24,152},{32,160},{40,168},{48,176},{56,1... | collective-permute-start | bytes 1253384 | tf_op jit(solution)/shard_map/ppermute | solution.py:374
  32.1 41.2 %collective-permute-start.9 = (bf16[272,768]{1,0:T(8,128)(2,1)}, bf16[272,768]{1,0:T(8,128)(2,1)S(1)}, u32[]{:S(2)}, u32[]{:S(2)}) collective-permute-start(bf16[272,768]{1,0:T(8,128)(2,1)} %collective-permute-done.refs_3_.refs_4_), channel_id=1, source_target_pairs={{0,16},{8,24},{16,32},{24,40},{32,48},{40,56},{48,64},{56,72},{64,... | collective-permute-start | bytes 1253384 | tf_op jit(solution)/shard_map/ppermute | solution.py:374
  34.3 82.0 %collective-permute-start.17 = (bf16[384,768]{1,0:T(8,128)(2,1)S(1)}, bf16[384,768]{1,0:T(8,128)(2,1)S(1)}, u32[]{:S(2)}, u32[]{:S(2)}) collective-permute-start(bf16[384,768]{1,0:T(8,128)(2,1)S(1)} %get-tuple-element.42), channel_id=1, source_target_pairs={{0,4},{1,5},{2,6},{3,7},{4,0},{5,1},{6,2},{7,3},{8,12},{9,13},{10,... | collective-permute-start | bytes 1769480 | tf_op jit(solution)/shard_map/ppermute | solution.py:382
  73.3 44.6 %collective-permute-start.11 = (bf16[272,768]{1,0:T(8,128)(2,1)S(1)}, bf16[272,768]{1,0:T(8,128)(2,1)S(1)}, u32[]{:S(2)}, u32[]{:S(2)}) collective-permute-start(bf16[272,768]{1,0:T(8,128)(2,1)S(1)} %collective-permute-done.9.refs_2_.refs_7_), channel_id=1, source_target_pairs={{0,16},{8,24},{16,32},{24,40},{32,48},{40,56},{48,64},{56,72},{64,... | collective-permute-start | bytes 1253384 | tf_op jit(solution)/shard_map/ppermute | solution.py:374
  73.4 44.5 %collective-permute-start.12 = (bf16[272,768]{1,0:T(8,128)(2,1)S(1)}, bf16[272,768]{1,0:T(8,128)(2,1)S(1)}, u32[]{:S(2)}, u32[]{:S(2)}) collective-permute-start(bf16[272,768]{1,0:T(8,128)(2,1)S(1)} %collective-permute-done.10.refs_3_.refs_8_), channel_id=1, source_target_pairs={{0,112},{8,120},{16,0},{24,8},{32,16},{40,24},{48,32},{56,40},{64,... | collective-permute-start | bytes 1253384 | tf_op jit(solution)/shard_map/ppermute | solution.py:374
  76.7 46.2 %collective-permute-start.2 = (bf16[272,768]{1,0:T(8,128)(2,1)S(1)}, bf16[272,768]{1,0:T(8,128)(2,1)S(1)}, u32[]{:S(2)}, u32[]{:S(2)}) collective-permute-start(bf16[272,768]{1,0:T(8,128)(2,1)S(1)} %collective-permute-done.1.refs_4_.refs_9_), channel_id=1, source_target_pairs={{0,16},{8,24},{16,32},{24,40},{32,48},{40,56},{48,64},{56,72},{64,... | collective-permute-start | bytes 1253384 | tf_op jit(solution)/shard_map/ppermute | solution.py:374
  76.7 46.2 %collective-permute-start.6 = (bf16[272,768]{1,0:T(8,128)(2,1)S(1)}, bf16[272,768]{1,0:T(8,128)(2,1)S(1)}, u32[]{:S(2)}, u32[]{:S(2)}) collective-permute-start(bf16[272,768]{1,0:T(8,128)(2,1)S(1)} %collective-permute-done.5.refs_5_.refs_10_), channel_id=1, source_target_pairs={{0,112},{8,120},{16,0},{24,8},{32,16},{40,24},{48,32},{56,40},{64,... | collective-permute-start | bytes 1253384 | tf_op jit(solution)/shard_map/ppermute | solution.py:374
  116.9 76.2 %collective-permute-start.18 = (bf16[384,768]{1,0:T(8,128)(2,1)S(1)}, bf16[384,768]{1,0:T(8,128)(2,1)S(1)}, u32[]{:S(2)}, u32[]{:S(2)}) collective-permute-start(bf16[384,768]{1,0:T(8,128)(2,1)S(1)} %columns.3), channel_id=1, source_target_pairs={{0,2},{1,3},{2,4},{3,5},{4,6},{5,7},{6,0},{7,1},{8,10},{9,11},{10,... | collective-permute-start | bytes 1769480 | tf_op jit(solution)/shard_map/ppermute | solution.py:382
  117.9 44.4 %collective-permute-start.13 = (bf16[272,768]{1,0:T(8,128)(2,1)S(1)}, bf16[272,768]{1,0:T(8,128)(2,1)S(1)}, u32[]{:S(2)}, u32[]{:S(2)}) collective-permute-start(bf16[272,768]{1,0:T(8,128)(2,1)S(1)} %collective-permute-done.11.refs_2_.refs_11_), channel_id=1, source_target_pairs={{0,16},{8,24},{16,32},{24,40},{32,48},{40,56},{48,64},{56,72},{64,... | collective-permute-start | bytes 1253384 | tf_op jit(solution)/shard_map/ppermute | solution.py:374
  117.9 44.4 %collective-permute-start.14 = (bf16[272,768]{1,0:T(8,128)(2,1)S(1)}, bf16[272,768]{1,0:T(8,128)(2,1)S(1)}, u32[]{:S(2)}, u32[]{:S(2)}) collective-permute-start(bf16[272,768]{1,0:T(8,128)(2,1)S(1)} %collective-permute-done.12.refs_3_.refs_12_), channel_id=1, source_target_pairs={{0,240},{8,248},{16,128},{24,136},{32,144},{40,152},{48,160},{56,1... | collective-permute-start | bytes 1253384 | tf_op jit(solution)/shard_map/ppermute | solution.py:374
  122.9 70.2 %collective-permute-start.3 = (bf16[272,768]{1,0:T(8,128)(2,1)S(1)}, bf16[272,768]{1,0:T(8,128)(2,1)S(1)}, u32[]{:S(2)}, u32[]{:S(2)}) collective-permute-start(bf16[272,768]{1,0:T(8,128)(2,1)S(1)} %collective-permute-done.2.refs_4_.refs_13_), channel_id=1, source_target_pairs={{0,16},{8,24},{16,32},{24,40},{32,48},{40,56},{48,64},{56,72},{64,... | collective-permute-start | bytes 1253384 | tf_op jit(solution)/shard_map/ppermute | solution.py:374
  122.9 70.2 %collective-permute-start.7 = (bf16[272,768]{1,0:T(8,128)(2,1)S(1)}, bf16[272,768]{1,0:T(8,128)(2,1)S(1)}, u32[]{:S(2)}, u32[]{:S(2)}) collective-permute-start(bf16[272,768]{1,0:T(8,128)(2,1)S(1)} %collective-permute-done.6.refs_5_.refs_14_), channel_id=1, source_target_pairs={{0,112},{8,120},{16,0},{24,8},{32,16},{40,24},{48,32},{56,40},{64,... | collective-permute-start | bytes 1253384 | tf_op jit(solution)/shard_map/ppermute | solution.py:374
  212.4 17.3 %collective-permute-start.19 = (bf16[3,144,1024]{2,1,0:T(8,128)(2,1)S(1)}, bf16[3,144,1024]{2,1,0:T(8,128)(2,1)S(1)}, u32[]{:S(2)}, u32[]{:S(2)}) collective-permute-start(bf16[3,144,1024]{2,1,0:T(8,128)(2,1)S(1)} %get-tuple-element.63), channel_id=1, source_target_pairs={{0,8},{8,0},{16,24},{24,16},{32,40},{40,32},{48,56},{56,48},{64,72... | collective-permute-start | bytes 2654216 | tf_op jit(solution)/shard_map/ppermute | solution.py:374
  233.3 13.2 %collective-permute-start.25 = (bf16[480,384]{1,0:T(8,128)(2,1)S(1)}, bf16[480,384]{1,0:T(8,128)(2,1)S(1)}, u32[]{:S(2)}, u32[]{:S(2)}) collective-permute-start(bf16[480,384]{1,0:T(8,128)(2,1)S(1)} %get-tuple-element.65.lower_ref.refs_1_), channel_id=1, source_target_pairs={{0,2},{1,3},{2,4},{3,5},{4,6},{5,7},{6,0},{7,1},{8,10},{9,11},{10,... | collective-permute-start | bytes 1105928 | tf_op jit(solution)/shard_map/ppermute | solution.py:382
  233.3 20.5 %collective-permute-start.21 = (bf16[480,384]{1,0:T(8,128)(2,1)S(1)}, bf16[480,384]{1,0:T(8,128)(2,1)S(1)}, u32[]{:S(2)}, u32[]{:S(2)}) collective-permute-start(bf16[480,384]{1,0:T(8,128)(2,1)S(1)} %get-tuple-element.64.upper_ref), channel_id=1, source_target_pairs={{0,2},{1,3},{2,4},{3,5},{4,6},{5,7},{6,0},{7,1},{8,10},{9,11},{10,... | collective-permute-start | bytes 1105928 | tf_op jit(solution)/shard_map/ppermute | solution.py:382
  246.4 14.7 %collective-permute-start.24 = (bf16[480,384]{1,0:T(8,128)(2,1)S(1)}, bf16[480,384]{1,0:T(8,128)(2,1)S(1)}, u32[]{:S(2)}, u32[]{:S(2)}) collective-permute-start(bf16[480,384]{1,0:T(8,128)(2,1)S(1)} %get-tuple-element.71), channel_id=1, source_target_pairs={{0,6},{1,7},{2,0},{3,1},{4,2},{5,3},{6,4},{7,5},{8,14},{9,15},{10,... | collective-permute-start | bytes 1105928 | tf_op jit(solution)/shard_map/ppermute | solution.py:382
  246.5 15.7 %collective-permute-start.26 = (bf16[480,384]{1,0:T(8,128)(2,1)S(1)}, bf16[480,384]{1,0:T(8,128)(2,1)S(1)}, u32[]{:S(2)}, u32[]{:S(2)}) collective-permute-start(bf16[480,384]{1,0:T(8,128)(2,1)S(1)} %collective-permute-done.25.two_ref.refs_3_), channel_id=1, source_target_pairs={{0,2},{1,3},{2,4},{3,5},{4,6},{5,7},{6,0},{7,1},{8,10},{9,11},{10,... | collective-permute-start | bytes 1105928 | tf_op jit(solution)/shard_map/ppermute | solution.py:382
  256.2 16.3 %collective-permute-start.23 = (bf16[480,384]{1,0:T(8,128)(2,1)S(1)}, bf16[480,384]{1,0:T(8,128)(2,1)S(1)}, u32[]{:S(2)}, u32[]{:S(2)}) collective-permute-start(bf16[480,384]{1,0:T(8,128)(2,1)S(1)} %get-tuple-element.69), channel_id=1, source_target_pairs={{0,1},{1,0},{2,3},{3,2},{4,5},{5,4},{6,7},{7,6},{8,9},{9,8},{10,11... | collective-permute-start | bytes 1105928 | tf_op jit(solution)/shard_map/ppermute | solution.py:382
  (18 other events, 189.5 us)
where the time goes:
time: 294 us; the launch traced here: 288 us
  Pallas kernels  188 us (64%)
  starting transfers between devices  53.8 us (18%)
  waiting for transfers between devices  37.6 us (13%)
  local copies, waits for them, and re-layouts  4.06 us (1%)
  other arithmetic  3.65 us (1%)
    pallas_call x6, Pallas kernels, attend(): pl.pallas_call(functools.partial(attend_kernel, groups, n, texts, first,...  177 us
    ppermute x17, starting transfers between devices, over_seq(): return lambda value: lax.ppermute(value, 'seq', pairs)  31 us
    ppermute x15, waiting for transfers between devices, over_head(): return lambda value: lax.ppermute(value, 'head', pairs)  30.7 us
    ppermute x15, starting transfers between devices, over_head(): return lambda value: lax.ppermute(value, 'head', pairs)  22.8 us
    ppermute x17, waiting for transfers between devices, over_seq(): return lambda value: lax.ppermute(value, 'seq', pairs)  6.88 us
  transfers between devices with their start and end apart: 32, of which 8 were waited for; matrix products, arithmetic and copies ran while one was open for 2% of the time, Pallas kernels for 57%

commit v1 on v0

--- a/solution.py
+++ b/solution.py
@@ -31,8 +31,8 @@
 HBM = pl.BlockSpec(memory_space=pltpu.HBM)
 
 
-def params():
-    return pltpu.CompilerParams(vmem_limit_bytes=30 * 2**20)
+def params(mib=30):
+    return pltpu.CompilerParams(vmem_limit_bytes=mib * 2**20)
 
 
 def with_ones(v):
@@ -88,17 +88,17 @@
             pairs.append(text_operands(h))
         for g in range(groups):
             q = q_refs[g][:, key_at]
-            if first:
-                top = jnp.max(scores_of(keys[0][:32], q), axis=0, keepdims=True)
-            else:
-                top = before[2 * g + 1][h, :1]
+            top = jnp.zeros((1, q.shape[0]), F32) if first else before[2 * g + 1][h, :1]
             total = None
             for k, v in pairs:
                 p = jnp.exp2(scores_of(jnp.concatenate(k, axis=0), q) - top).astype(BF16)
                 d = jnp.dot(with_ones(jnp.concatenate(v, axis=0)), p, preferred_element_type=F32)
                 total = d if total is None else total + d
             added[g, h], tops[g, h] = total, top
-    fine = jnp.max(jnp.concatenate([a[DH : DH + 1] for a in added.values()], axis=1)) < LIMIT
+    totals = jnp.concatenate([a[DH : DH + 1] for a in added.values()], axis=1)
+    fine = jnp.max(totals) < LIMIT
+    if first:
+        fine = jnp.logical_and(fine, jnp.min(totals) > 1e-20)
 
     @pl.when(fine)
     def _():
@@ -248,7 +248,7 @@
         out_specs=[VMEM] * len(steps),
         out_shape=[jax.ShapeDtypeStruct((WIDTH, 2 * WIDTH), BF16)] * len(steps),
         scratch_shapes=[pltpu.SemaphoreType.DMA(())] * len(steps),
-        compiler_params=params(),
+        compiler_params=params(61 if len(steps) > 1 else 30),
         name="columns",
     )(at, weight, *unread)
 
@@ -410,9 +410,9 @@
     r4, opposite = up(r3), across(l3)
     ry3, ly3 = up(ry2), down(ly2)
 
-    slice_1 = lax.dynamic_slice_in_dim(out_video, lax.rem(x_at + 3, 4) * 2 * WIDTH, 2 * WIDTH, axis=1)
+    here, slice_1 = column_slices(at, out_video, (0, 1), unread=[own])
     weight_1 = from_on[1](slice_1)
-    here, slice_2 = column_slices(at, out_video, (0, 2), unread=[weight_1])
+    [slice_2] = column_slices(at, out_video, (2,), unread=[y0, weight_1])
     weight_2 = from_on[2](slice_2)
     [slice_3] = column_slices(at, out_video, (3,), unread=[weight_2])
     weights = [here, weight_1, weight_2, from_on[3](slice_3)]
@@ -421,8 +421,8 @@
         [q_other[:VID], q_text, q_other[VID:], jnp.zeros((THEIRS - VID - 2 * TXTR, WIDTH), BF16)], axis=0
     )
     queries = [q_theirs, q_video]
-    states = attend(queries, [own, r1, l1, y0])
-    states = attend(queries, [r2, l2, yr1, yl1], states, unread=weights[1:2])
+    states = attend(queries, [own, r1, l1, y0], unread=weights[1:2])
+    states = attend(queries, [r2, l2, yr1, yl1], states)
     states = attend(queries, [r3, l3, ry2, ly2], states, unread=weights[2:3])
     states = attend(queries, [r4, opposite], states)
     every = [ry3, ly3, own, r1, l1, y0, r2, l2, yr1, yl1, r3, l3, ry2, ly2, r4, opposite]

time: 294 us -> 291 us (0.990)
    pallas_call x6, Pallas kernels: 177 us -> 173 us  [attend(): pl.pallas_call(functools.partial(attend_kernel, groups, n, texts, first,...]
    pallas_call x2 -> x3, Pallas kernels: 1.3 us -> 4.3 us  [column_slices(): pl.pallas_call(functools.partial(slice_kernel, steps, len(unread)), in_sp...]
where the time goes in v1:
time: 291 us; the launch traced here: 286 us
  Pallas kernels  186 us (64%)
  starting transfers between devices  53.7 us (18%)
  waiting for transfers between devices  37.8 us (13%)
  other arithmetic  4.86 us (2%)
    pallas_call x6, Pallas kernels, attend(): pl.pallas_call(functools.partial(attend_kernel, groups, n, texts, first,...  173 us
    ppermute x15, waiting for transfers between devices, over_head(): return lambda value: lax.ppermute(value, 'head', pairs)  30.8 us
    ppermute x17, starting transfers between devices, over_seq(): return lambda value: lax.ppermute(value, 'seq', pairs)  30.6 us
    ppermute x15, starting transfers between devices, over_head(): return lambda value: lax.ppermute(value, 'head', pairs)  23.1 us
    ppermute x17, waiting for transfers between devices, over_seq(): return lambda value: lax.ppermute(value, 'seq', pairs)  6.95 us
  transfers between devices with their start and end apart: 32, of which 8 were waited for; matrix products, arithmetic and copies ran while one was open for 2% of the time, Pallas kernels for 57%

profile of v1, /device:TPU:8, one launch (start us, length us, event | category | flops | bytes accessed | tf_op | source)
XLA Modules:
  0.0 286.0 jit_solution(5334681537668119301)
XLA Ops:
  5.4 3.1 %columns.3 = (bf16[384,768]{1,0:T(8,128)(2,1)}, bf16[384,768]{1,0:T(8,128)(2,1)}) custom-call(s32[2]{0:T(128)} %pad_add_fusion.at_ref, bf16[384,3072]{1,0:T(8,128)(2,1)} %w_ref.5, bf16[272,768]{1,0:T(8,128)(2,1)} %maximum_maximum_fusion.1.refs_0_.refs_2_.refs_3_), custom_call_target="tpu_custom_call" | custom-call | tf_op jit(solution)/shard_map/columns/pallas_call | solution.py:245
  8.4 2.8 collective-permute-start.16
  11.3 5.9 %collective-permute-start.4 = (bf16[272,768]{1,0:T(8,128)(2,1)S(1)}, bf16[272,768]{1,0:T(8,128)(2,1)S(1)}, u32[]{:S(2)}, u32[]{:S(2)}) collective-permute-start(bf16[272,768]{1,0:T(8,128)(2,1)S(1)} %copy-done.1), channel_id=1, source_target_pairs={{0,112},{8,120},{16,0},{24,8},{32,16},{40,24},{48,32},{56,40},{64,... | collective-permute-start | bytes 1253384 | tf_op jit(solution)/shard_map/ppermute | solution.py:374
  19.5 6.9 %collective-permute-done.4.refs_4_.refs_5_ = bf16[272,768]{1,0:T(8,128)(2,1)S(1)} collective-permute-done((bf16[272,768]{1,0:T(8,128)(2,1)S(1)}, bf16[272,768]{1,0:T(8,128)(2,1)S(1)}, u32[]{:S(2)}, u32[]{:S(2)}) %collective-permute-start.4) | collective-permute-done | bytes 417824 | tf_op jit(solution)/shard_map/ppermute | solution.py:374
  26.4 3.7 %collective-permute-start.10 = (bf16[272,768]{1,0:T(8,128)(2,1)S(1)}, bf16[272,768]{1,0:T(8,128)(2,1)S(1)}, u32[]{:S(2)}, u32[]{:S(2)}) collective-permute-start(bf16[272,768]{1,0:T(8,128)(2,1)S(1)} %collective-permute-done.4.refs_4_.refs_5_), channel_id=1, source_target_pairs={{0,112},{8,120},{16,0},{24,8},{32,16},{40,24},{48,32},{56,40},{64,... | collective-permute-start | bytes 1253384 | tf_op jit(solution)/shard_map/ppermute | solution.py:374
  37.8 36.0 %attend.6 = (f32[3,144,1024]{2,1,0:T(8,128)S(1)}, f32[3,8,1024]{2,1,0:T(8,128)S(1)}, f32[3,144,896]{2,1,0:T(8,128)S(1)}, f32[3,8,896]{2,1,0:T(8,128)S(1)}) custom-call(bf16[1024,384]{1,0:T(8,128)(2,1)S(1)} %maximum_maximum_fusion.refs_0_, bf16[896,384]{1,0:T(8,128)(2,1)S(1)} %copy-done.2, bf16[272,768]{1,0:T(8,128)(2,1)S(1)} %copy-done.1, ...), custom_call_target="tpu_custom_call" | custom-call | flops 6039797760 | bytes 3317760 | tf_op jit(solution)/shard_map/attend/pallas_call | solution.py:165
  74.0 3.3 %collective-permute-start.12 = (bf16[272,768]{1,0:T(8,128)(2,1)S(1)}, bf16[272,768]{1,0:T(8,128)(2,1)S(1)}, u32[]{:S(2)}, u32[]{:S(2)}) collective-permute-start(bf16[272,768]{1,0:T(8,128)(2,1)S(1)} %collective-permute-done.10.refs_3_.refs_8_), channel_id=1, source_target_pairs={{0,112},{8,120},{16,0},{24,8},{32,16},{40,24},{48,32},{56,40},{64,... | collective-permute-start | bytes 1253384 | tf_op jit(solution)/shard_map/ppermute | solution.py:374
  77.3 3.4 %collective-permute-start.6 = (bf16[272,768]{1,0:T(8,128)(2,1)S(1)}, bf16[272,768]{1,0:T(8,128)(2,1)S(1)}, u32[]{:S(2)}, u32[]{:S(2)}) collective-permute-start(bf16[272,768]{1,0:T(8,128)(2,1)S(1)} %collective-permute-done.5.refs_5_.refs_10_), channel_id=1, source_target_pairs={{0,112},{8,120},{16,0},{24,8},{32,16},{40,24},{48,32},{56,40},{64,... | collective-permute-start | bytes 1253384 | tf_op jit(solution)/shard_map/ppermute | solution.py:374
  80.7 36.1 %attend.7 = (f32[3,144,1024]{2,1,0:T(8,128)S(1)}, f32[3,8,1024]{2,1,0:T(8,128)S(1)}, f32[3,144,896]{2,1,0:T(8,128)S(1)}, f32[3,8,896]{2,1,0:T(8,128)S(1)}) custom-call(bf16[1024,384]{1,0:T(8,128)(2,1)S(1)} %maximum_maximum_fusion.refs_0_, bf16[896,384]{1,0:T(8,128)(2,1)S(1)} %copy-done.2, ...), custom_call_target="tpu_custom_call", output_to_operand_aliasing={{0}: (6, {}), {1}: (7, {}), {2}: (8, {}), {3}: (9, {})} | custom-call | flops 6039797760 | bytes 3317760 | tf_op jit(solution)/shard_map/attend/pallas_call | solution.py:165
  118.4 5.0 %collective-permute-start.14 = (bf16[272,768]{1,0:T(8,128)(2,1)S(1)}, bf16[272,768]{1,0:T(8,128)(2,1)S(1)}, u32[]{:S(2)}, u32[]{:S(2)}) collective-permute-start(bf16[272,768]{1,0:T(8,128)(2,1)S(1)} %collective-permute-done.12.refs_3_.refs_12_), channel_id=1, source_target_pairs={{0,240},{8,248},{16,128},{24,136},{32,144},{40,152},{48,160},{56,1... | collective-permute-start | bytes 1253384 | tf_op jit(solution)/shard_map/ppermute | solution.py:374
  123.4 3.4 %collective-permute-start.7 = (bf16[272,768]{1,0:T(8,128)(2,1)S(1)}, bf16[272,768]{1,0:T(8,128)(2,1)S(1)}, u32[]{:S(2)}, u32[]{:S(2)}) collective-permute-start(bf16[272,768]{1,0:T(8,128)(2,1)S(1)} %collective-permute-done.6.refs_5_.refs_14_), channel_id=1, source_target_pairs={{0,112},{8,120},{16,0},{24,8},{32,16},{40,24},{48,32},{56,40},{64,... | collective-permute-start | bytes 1253384 | tf_op jit(solution)/shard_map/ppermute | solution.py:374
  126.8 36.0 %attend.8 = (f32[3,144,1024]{2,1,0:T(8,128)S(1)}, f32[3,8,1024]{2,1,0:T(8,128)S(1)}, f32[3,144,896]{2,1,0:T(8,128)S(1)}, f32[3,8,896]{2,1,0:T(8,128)S(1)}) custom-call(bf16[1024,384]{1,0:T(8,128)(2,1)S(1)} %maximum_maximum_fusion.refs_0_, bf16[896,384]{1,0:T(8,128)(2,1)S(1)} %copy-done.2, ...), custom_call_target="tpu_custom_call", output_to_operand_aliasing={{0}: (7, {}), {1}: (8, {}), {2}: (9, {}), {3}: (10, {})} | custom-call | flops 6039797760 | bytes 3317760 | tf_op jit(solution)/shard_map/attend/pallas_call | solution.py:165
  162.8 30.9 %attend.9 = (f32[3,144,1024]{2,1,0:T(8,128)S(1)}, f32[3,8,1024]{2,1,0:T(8,128)S(1)}, f32[3,144,896]{2,1,0:T(8,128)S(1)}, f32[3,8,896]{2,1,0:T(8,128)S(1)}) custom-call(bf16[1024,384]{1,0:T(8,128)(2,1)S(1)} %maximum_maximum_fusion.refs_0_, bf16[896,384]{1,0:T(8,128)(2,1)S(1)} %copy-done.2, ...), custom_call_target="tpu_custom_call", output_to_operand_aliasing={{0}: (4, {}), {1}: (5, {}), {2}: (6, {}), {3}: (7, {})} | custom-call | flops 3019898880 | bytes 3317760 | tf_op jit(solution)/shard_map/attend/pallas_call | solution.py:165
  193.8 18.0 %attend.11 = (f32[3,144,1024]{2,1,0:T(8,128)S(1)}, f32[3,8,1024]{2,1,0:T(8,128)S(1)}, bf16[3,144,1024]{2,1,0:T(8,128)(2,1)S(1)}) custom-call(bf16[1024,384]{1,0:T(8,128)(2,1)S(1)} %maximum_maximum_fusion.refs_0_, bf16[272,768]{1,0:T(8,128)(2,1)S(1)} %collective-permute-done.3.refs_1_, ...), custom_call_target="tpu_custom_call", output_to_operand_aliasing={{0}: (18, {}), {1}: (19, {})} | custom-call | flops 2013265920 | bytes 1769472 | tf_op jit(solution)/shard_map/attend/pallas_call | solution.py:165
  211.9 15.7 %attend.10 = (f32[3,144,896]{2,1,0:T(8,128)S(1)}, f32[3,8,896]{2,1,0:T(8,128)S(1)}) custom-call(bf16[896,384]{1,0:T(8,128)(2,1)S(1)} %copy-done.2, bf16[272,768]{1,0:T(8,128)(2,1)S(1)} %collective-permute-done.3.refs_1_, bf16[272,768]{1,0:T(8,128)(2,1)S(1)} %collective-permute-done.7.refs_2_, ...), custom_call_target="tpu_custom_call", output_to_operand_aliasing={{0}: (17, {}), {1}: (18, {})} | custom-call | flops 1761607680 | bytes 1548288 | tf_op jit(solution)/shard_map/attend/pallas_call | solution.py:165
  228.9 2.4 collective-permute-start.20
  232.8 7.2 %collective-permute-done.20.arrived_ref.one_ref = bf16[480,384]{1,0:T(8,128)(2,1)S(1)} collective-permute-done((bf16[480,384]{1,0:T(8,128)(2,1)S(1)}, bf16[480,384]{1,0:T(8,128)(2,1)S(1)}, u32[]{:S(2)}, u32[]{:S(2)}) %collective-permute-start.20) | collective-permute-done | bytes 368672 | tf_op jit(solution)/shard_map/ppermute | solution.py:382
  240.0 3.5 %collective-permute-start.22 = (bf16[480,384]{1,0:T(8,128)(2,1)S(1)}, bf16[480,384]{1,0:T(8,128)(2,1)S(1)}, u32[]{:S(2)}, u32[]{:S(2)}) collective-permute-start(bf16[480,384]{1,0:T(8,128)(2,1)S(1)} %collective-permute-done.20.arrived_ref.one_ref), channel_id=1, source_target_pairs={{0,6},{1,7},{2,0},{3,1},{4,2},{5,3},{6,4},{7,5},{8,14},{9,15},{10,... | collective-permute-start | bytes 1105928 | tf_op jit(solution)/shard_map/ppermute | solution.py:382
  246.6 5.2 %collective-permute-done.21.two_ref = bf16[480,384]{1,0:T(8,128)(2,1)S(1)} collective-permute-done((bf16[480,384]{1,0:T(8,128)(2,1)S(1)}, bf16[480,384]{1,0:T(8,128)(2,1)S(1)}, u32[]{:S(2)}, u32[]{:S(2)}) %collective-permute-start.21) | collective-permute-done | bytes 368672 | tf_op jit(solution)/shard_map/ppermute | solution.py:382
  255.6 3.5 %collective-permute-done.24.one_ref.refs_2_ = bf16[480,384]{1,0:T(8,128)(2,1)S(1)} collective-permute-done((bf16[480,384]{1,0:T(8,128)(2,1)S(1)}, bf16[480,384]{1,0:T(8,128)(2,1)S(1)}, u32[]{:S(2)}, u32[]{:S(2)}) %collective-permute-start.24) | collective-permute-done | bytes 368672 | tf_op jit(solution)/shard_map/ppermute | solution.py:382
  262.7 7.8 %collective-permute-done.27.got_b = bf16[432,384]{1,0:T(8,128)(2,1)S(1)} collective-permute-done((bf16[432,384]{1,0:T(8,128)(2,1)S(1)}, bf16[432,384]{1,0:T(8,128)(2,1)S(1)}, u32[]{:S(2)}, u32[]{:S(2)}) %collective-permute-start.27) | collective-permute-done | bytes 331808 | tf_op jit(solution)/shard_map/ppermute | solution.py:382
  273.1 2.6 collective-permute-done.28
  275.6 3.1 %collective-permute-start.29 = (f32[8,1024]{1,0:T(8,128)S(1)}, f32[8,1024]{1,0:T(8,128)S(1)}, u32[]{:S(2)}, u32[]{:S(2)}) collective-permute-start(f32[8,1024]{1,0:T(8,128)S(1)} %add.9.s0_ref), channel_id=1, source_target_pairs={{0,6},{1,7},{2,0},{3,1},{4,2},{5,3},{6,4},{7,5},{8,14},{9,15},{10,... | collective-permute-start | bytes 98312 | tf_op jit(solution)/shard_map/ppermute | solution.py:382
  280.3 3.9 %collective-permute-done.30.s2_ref = f32[8,1024]{1,0:T(8,128)S(1)} collective-permute-done((f32[8,1024]{1,0:T(8,128)S(1)}, f32[8,1024]{1,0:T(8,128)S(1)}, u32[]{:S(2)}, u32[]{:S(2)}) %collective-permute-start.30) | collective-permute-done | bytes 32800 | tf_op jit(solution)/shard_map/ppermute | solution.py:382
  (90 shorter events, 35.4 us)
Async XLA Ops:
  2.7 31.6 %collective-permute-start.15 = (bf16[904,384]{1,0:T(8,128)(2,1)}, bf16[904,384]{1,0:T(8,128)(2,1)}, u32[]{:S(2)}, u32[]{:S(2)}) collective-permute-start(bf16[904,384]{1,0:T(8,128)(2,1)} %pad_maximum_fusion), channel_id=1, source_target_pairs={{0,8},{8,0},{16,24},{24,16},{32,40},{40,32},{48,56},{56,48},{64,72... | collective-permute-start | bytes 2082824 | tf_op jit(solution)/shard_map/ppermute | solution.py:374
  8.4 25.2 %collective-permute-start.16 = (bf16[384,768]{1,0:T(8,128)(2,1)}, bf16[384,768]{1,0:T(8,128)(2,1)S(1)}, u32[]{:S(2)}, u32[]{:S(2)}) collective-permute-start(bf16[384,768]{1,0:T(8,128)(2,1)} %get-tuple-element.42), channel_id=1, source_target_pairs={{0,6},{1,7},{2,0},{3,1},{4,2},{5,3},{6,4},{7,5},{8,14},{9,15},{10,... | collective-permute-start | bytes 1769480 | tf_op jit(solution)/shard_map/ppermute | solution.py:382
  11.3 15.1 %collective-permute-start.4 = (bf16[272,768]{1,0:T(8,128)(2,1)S(1)}, bf16[272,768]{1,0:T(8,128)(2,1)S(1)}, u32[]{:S(2)}, u32[]{:S(2)}) collective-permute-start(bf16[272,768]{1,0:T(8,128)(2,1)S(1)} %copy-done.1), channel_id=1, source_target_pairs={{0,112},{8,120},{16,0},{24,8},{32,16},{40,24},{48,32},{56,40},{64,... | collective-permute-start | bytes 1253384 | tf_op jit(solution)/shard_map/ppermute | solution.py:374
  17.1 15.3 %collective-permute-start.8 = (bf16[272,768]{1,0:T(8,128)(2,1)S(1)}, bf16[272,768]{1,0:T(8,128)(2,1)S(1)}, u32[]{:S(2)}, u32[]{:S(2)}) collective-permute-start(bf16[272,768]{1,0:T(8,128)(2,1)S(1)} %copy-done.1), channel_id=1, source_target_pairs={{0,128},{8,136},{16,144},{24,152},{32,160},{40,168},{48,176},{56,1... | collective-permute-start | bytes 1253384 | tf_op jit(solution)/shard_map/ppermute | solution.py:374
  26.4 47.6 %collective-permute-start.10 = (bf16[272,768]{1,0:T(8,128)(2,1)S(1)}, bf16[272,768]{1,0:T(8,128)(2,1)S(1)}, u32[]{:S(2)}, u32[]{:S(2)}) collective-permute-start(bf16[272,768]{1,0:T(8,128)(2,1)S(1)} %collective-permute-done.4.refs_4_.refs_5_), channel_id=1, source_target_pairs={{0,112},{8,120},{16,0},{24,8},{32,16},{40,24},{48,32},{56,40},{64,... | collective-permute-start | bytes 1253384 | tf_op jit(solution)/shard_map/ppermute | solution.py:374
  30.1 47.2 %collective-permute-start.5 = (bf16[272,768]{1,0:T(8,128)(2,1)S(1)}, bf16[272,768]{1,0:T(8,128)(2,1)S(1)}, u32[]{:S(2)}, u32[]{:S(2)}) collective-permute-start(bf16[272,768]{1,0:T(8,128)(2,1)S(1)} %collective-permute-done.4.refs_4_.refs_5_), channel_id=1, source_target_pairs={{0,128},{8,136},{16,144},{24,152},{32,160},{40,168},{48,176},{56,1... | collective-permute-start | bytes 1253384 | tf_op jit(solution)/shard_map/ppermute | solution.py:374
  32.4 44.9 %collective-permute-start.1 = (bf16[272,768]{1,0:T(8,128)(2,1)S(1)}, bf16[272,768]{1,0:T(8,128)(2,1)S(1)}, u32[]{:S(2)}, u32[]{:S(2)}) collective-permute-start(bf16[272,768]{1,0:T(8,128)(2,1)S(1)} %collective-permute-done.refs_3_.refs_4_), channel_id=1, source_target_pairs={{0,128},{8,136},{16,144},{24,152},{32,160},{40,168},{48,176},{56,1... | collective-permute-start | bytes 1253384 | tf_op jit(solution)/shard_map/ppermute | solution.py:374
  33.7 40.2 %collective-permute-start.9 = (bf16[272,768]{1,0:T(8,128)(2,1)S(1)}, bf16[272,768]{1,0:T(8,128)(2,1)S(1)}, u32[]{:S(2)}, u32[]{:S(2)}) collective-permute-start(bf16[272,768]{1,0:T(8,128)(2,1)S(1)} %collective-permute-done.refs_3_.refs_4_), channel_id=1, source_target_pairs={{0,16},{8,24},{16,32},{24,40},{32,48},{40,56},{48,64},{56,72},{64,... | collective-permute-start | bytes 1253384 | tf_op jit(solution)/shard_map/ppermute | solution.py:374
  34.3 82.4 %collective-permute-start.17 = (bf16[384,768]{1,0:T(8,128)(2,1)S(1)}, bf16[384,768]{1,0:T(8,128)(2,1)S(1)}, u32[]{:S(2)}, u32[]{:S(2)}) collective-permute-start(bf16[384,768]{1,0:T(8,128)(2,1)S(1)} %columns.4), channel_id=1, source_target_pairs={{0,4},{1,5},{2,6},{3,7},{4,0},{5,1},{6,2},{7,3},{8,12},{9,13},{10,... | collective-permute-start | bytes 1769480 | tf_op jit(solution)/shard_map/ppermute | solution.py:382
  73.9 44.5 %collective-permute-start.11 = (bf16[272,768]{1,0:T(8,128)(2,1)S(1)}, bf16[272,768]{1,0:T(8,128)(2,1)S(1)}, u32[]{:S(2)}, u32[]{:S(2)}) collective-permute-start(bf16[272,768]{1,0:T(8,128)(2,1)S(1)} %collective-permute-done.9.refs_2_.refs_7_), channel_id=1, source_target_pairs={{0,16},{8,24},{16,32},{24,40},{32,48},{40,56},{48,64},{56,72},{64,... | collective-permute-start | bytes 1253384 | tf_op jit(solution)/shard_map/ppermute | solution.py:374
  74.0 44.4 %collective-permute-start.12 = (bf16[272,768]{1,0:T(8,128)(2,1)S(1)}, bf16[272,768]{1,0:T(8,128)(2,1)S(1)}, u32[]{:S(2)}, u32[]{:S(2)}) collective-permute-start(bf16[272,768]{1,0:T(8,128)(2,1)S(1)} %collective-permute-done.10.refs_3_.refs_8_), channel_id=1, source_target_pairs={{0,112},{8,120},{16,0},{24,8},{32,16},{40,24},{48,32},{56,40},{64,... | collective-permute-start | bytes 1253384 | tf_op jit(solution)/shard_map/ppermute | solution.py:374
  77.3 46.0 %collective-permute-start.2 = (bf16[272,768]{1,0:T(8,128)(2,1)S(1)}, bf16[272,768]{1,0:T(8,128)(2,1)S(1)}, u32[]{:S(2)}, u32[]{:S(2)}) collective-permute-start(bf16[272,768]{1,0:T(8,128)(2,1)S(1)} %collective-permute-done.1.refs_4_.refs_9_), channel_id=1, source_target_pairs={{0,16},{8,24},{16,32},{24,40},{32,48},{40,56},{48,64},{56,72},{64,... | collective-permute-start | bytes 1253384 | tf_op jit(solution)/shard_map/ppermute | solution.py:374
  77.3 46.0 %collective-permute-start.6 = (bf16[272,768]{1,0:T(8,128)(2,1)S(1)}, bf16[272,768]{1,0:T(8,128)(2,1)S(1)}, u32[]{:S(2)}, u32[]{:S(2)}) collective-permute-start(bf16[272,768]{1,0:T(8,128)(2,1)S(1)} %collective-permute-done.5.refs_5_.refs_10_), channel_id=1, source_target_pairs={{0,112},{8,120},{16,0},{24,8},{32,16},{40,24},{48,32},{56,40},{64,... | collective-permute-start | bytes 1253384 | tf_op jit(solution)/shard_map/ppermute | solution.py:374
  117.4 76.4 %collective-permute-start.18 = (bf16[384,768]{1,0:T(8,128)(2,1)S(1)}, bf16[384,768]{1,0:T(8,128)(2,1)S(1)}, u32[]{:S(2)}, u32[]{:S(2)}) collective-permute-start(bf16[384,768]{1,0:T(8,128)(2,1)S(1)} %columns.5), channel_id=1, source_target_pairs={{0,2},{1,3},{2,4},{3,5},{4,6},{5,7},{6,0},{7,1},{8,10},{9,11},{10,... | collective-permute-start | bytes 1769480 | tf_op jit(solution)/shard_map/ppermute | solution.py:382
  118.4 44.4 %collective-permute-start.13 = (bf16[272,768]{1,0:T(8,128)(2,1)S(1)}, bf16[272,768]{1,0:T(8,128)(2,1)S(1)}, u32[]{:S(2)}, u32[]{:S(2)}) collective-permute-start(bf16[272,768]{1,0:T(8,128)(2,1)S(1)} %collective-permute-done.11.refs_2_.refs_11_), channel_id=1, source_target_pairs={{0,16},{8,24},{16,32},{24,40},{32,48},{40,56},{48,64},{56,72},{64,... | collective-permute-start | bytes 1253384 | tf_op jit(solution)/shard_map/ppermute | solution.py:374
  118.4 44.4 %collective-permute-start.14 = (bf16[272,768]{1,0:T(8,128)(2,1)S(1)}, bf16[272,768]{1,0:T(8,128)(2,1)S(1)}, u32[]{:S(2)}, u32[]{:S(2)}) collective-permute-start(bf16[272,768]{1,0:T(8,128)(2,1)S(1)} %collective-permute-done.12.refs_3_.refs_12_), channel_id=1, source_target_pairs={{0,240},{8,248},{16,128},{24,136},{32,144},{40,152},{48,160},{56,1... | collective-permute-start | bytes 1253384 | tf_op jit(solution)/shard_map/ppermute | solution.py:374
  123.3 70.4 %collective-permute-start.3 = (bf16[272,768]{1,0:T(8,128)(2,1)S(1)}, bf16[272,768]{1,0:T(8,128)(2,1)S(1)}, u32[]{:S(2)}, u32[]{:S(2)}) collective-permute-start(bf16[272,768]{1,0:T(8,128)(2,1)S(1)} %collective-permute-done.2.refs_4_.refs_13_), channel_id=1, source_target_pairs={{0,16},{8,24},{16,32},{24,40},{32,48},{40,56},{48,64},{56,72},{64,... | collective-permute-start | bytes 1253384 | tf_op jit(solution)/shard_map/ppermute | solution.py:374
  123.4 70.4 %collective-permute-start.7 = (bf16[272,768]{1,0:T(8,128)(2,1)S(1)}, bf16[272,768]{1,0:T(8,128)(2,1)S(1)}, u32[]{:S(2)}, u32[]{:S(2)}) collective-permute-start(bf16[272,768]{1,0:T(8,128)(2,1)S(1)} %collective-permute-done.6.refs_5_.refs_14_), channel_id=1, source_target_pairs={{0,112},{8,120},{16,0},{24,8},{32,16},{40,24},{48,32},{56,40},{64,... | collective-permute-start | bytes 1253384 | tf_op jit(solution)/shard_map/ppermute | solution.py:374
  211.8 15.9 %collective-permute-start.19 = (bf16[3,144,1024]{2,1,0:T(8,128)(2,1)S(1)}, bf16[3,144,1024]{2,1,0:T(8,128)(2,1)S(1)}, u32[]{:S(2)}, u32[]{:S(2)}) collective-permute-start(bf16[3,144,1024]{2,1,0:T(8,128)(2,1)S(1)} %get-tuple-element.63), channel_id=1, source_target_pairs={{0,8},{8,0},{16,24},{24,16},{32,40},{40,32},{48,56},{56,48},{64,72... | collective-permute-start | bytes 2654216 | tf_op jit(solution)/shard_map/ppermute | solution.py:374
  231.3 13.2 %collective-permute-start.25 = (bf16[480,384]{1,0:T(8,128)(2,1)S(1)}, bf16[480,384]{1,0:T(8,128)(2,1)S(1)}, u32[]{:S(2)}, u32[]{:S(2)}) collective-permute-start(bf16[480,384]{1,0:T(8,128)(2,1)S(1)} %get-tuple-element.65.lower_ref.refs_1_), channel_id=1, source_target_pairs={{0,2},{1,3},{2,4},{3,5},{4,6},{5,7},{6,0},{7,1},{8,10},{9,11},{10,... | collective-permute-start | bytes 1105928 | tf_op jit(solution)/shard_map/ppermute | solution.py:382
  231.3 20.5 %collective-permute-start.21 = (bf16[480,384]{1,0:T(8,128)(2,1)S(1)}, bf16[480,384]{1,0:T(8,128)(2,1)S(1)}, u32[]{:S(2)}, u32[]{:S(2)}) collective-permute-start(bf16[480,384]{1,0:T(8,128)(2,1)S(1)} %get-tuple-element.64.upper_ref), channel_id=1, source_target_pairs={{0,2},{1,3},{2,4},{3,5},{4,6},{5,7},{6,0},{7,1},{8,10},{9,11},{10,... | collective-permute-start | bytes 1105928 | tf_op jit(solution)/shard_map/ppermute | solution.py:382
  244.4 14.7 %collective-permute-start.24 = (bf16[480,384]{1,0:T(8,128)(2,1)S(1)}, bf16[480,384]{1,0:T(8,128)(2,1)S(1)}, u32[]{:S(2)}, u32[]{:S(2)}) collective-permute-start(bf16[480,384]{1,0:T(8,128)(2,1)S(1)} %get-tuple-element.71), channel_id=1, source_target_pairs={{0,6},{1,7},{2,0},{3,1},{4,2},{5,3},{6,4},{7,5},{8,14},{9,15},{10,... | collective-permute-start | bytes 1105928 | tf_op jit(solution)/shard_map/ppermute | solution.py:382
  244.5 15.7 %collective-permute-start.26 = (bf16[480,384]{1,0:T(8,128)(2,1)S(1)}, bf16[480,384]{1,0:T(8,128)(2,1)S(1)}, u32[]{:S(2)}, u32[]{:S(2)}) collective-permute-start(bf16[480,384]{1,0:T(8,128)(2,1)S(1)} %collective-permute-done.25.two_ref.refs_3_), channel_id=1, source_target_pairs={{0,2},{1,3},{2,4},{3,5},{4,6},{5,7},{6,0},{7,1},{8,10},{9,11},{10,... | collective-permute-start | bytes 1105928 | tf_op jit(solution)/shard_map/ppermute | solution.py:382
  254.2 16.3 %collective-permute-start.23 = (bf16[480,384]{1,0:T(8,128)(2,1)S(1)}, bf16[480,384]{1,0:T(8,128)(2,1)S(1)}, u32[]{:S(2)}, u32[]{:S(2)}) collective-permute-start(bf16[480,384]{1,0:T(8,128)(2,1)S(1)} %get-tuple-element.69), channel_id=1, source_target_pairs={{0,1},{1,0},{2,3},{3,2},{4,5},{5,4},{6,7},{7,6},{8,9},{9,8},{10,11... | collective-permute-start | bytes 1105928 | tf_op jit(solution)/shard_map/ppermute | solution.py:382
  (19 other events, 224.2 us)

commit v2 on v1

--- a/solution.py
+++ b/solution.py
@@ -31,8 +31,8 @@
 HBM = pl.BlockSpec(memory_space=pltpu.HBM)
 
 
-def params(mib=30):
-    return pltpu.CompilerParams(vmem_limit_bytes=mib * 2**20)
+def params():
+    return pltpu.CompilerParams(vmem_limit_bytes=30 * 2**20)
 
 
 def with_ones(v):
@@ -199,12 +199,12 @@
         video = merged(acc_ref[h], top_ref[h, :1], got_ref[h, :, :VID].astype(F32)).T.astype(BF16)
         upper_ref[:, at] = video[:UPPER]
         lower_ref[:LOWER, at] = video[UPPER:]
-        got = pltpu.roll(got_ref[h, :, VID:].astype(F32), DH - TXTR, 1)
+        got = pltpu.roll(got_ref[h, :, VID:].astype(F32), TXTR, 1)
         rows = merged(text_acc[h, :, VID:], text_top[h, :1, VID:], got).T
         rows_ref[:, at] = rows[: 2 * TXTR].astype(BF16)
 
     copy.wait()
-    part = jnp.dot(rows_ref[...], w_ref[...], preferred_element_type=F32)[:TXTR]
+    part = jnp.dot(rows_ref[...], w_ref[...], preferred_element_type=F32)[TXTR:]
     chunks = [part[:, j * WIDTH : (j + 1) * WIDTH] for j in range(CHUNKS)]
     lower_ref[LOWER:] = jnp.concatenate(chunks, axis=0).astype(BF16)
 
@@ -248,7 +248,7 @@
         out_specs=[VMEM] * len(steps),
         out_shape=[jax.ShapeDtypeStruct((WIDTH, 2 * WIDTH), BF16)] * len(steps),
         scratch_shapes=[pltpu.SemaphoreType.DMA(())] * len(steps),
-        compiler_params=params(61 if len(steps) > 1 else 30),
+        compiler_params=params(),
         name="columns",
     )(at, weight, *unread)
 
@@ -410,23 +410,21 @@
     r4, opposite = up(r3), across(l3)
     ry3, ly3 = up(ry2), down(ly2)
 
-    here, slice_1 = column_slices(at, out_video, (0, 1), unread=[own])
+    here, slice_1 = column_slices(at, out_video, (0, 1), unread=[q_other])
     weight_1 = from_on[1](slice_1)
     [slice_2] = column_slices(at, out_video, (2,), unread=[y0, weight_1])
     weight_2 = from_on[2](slice_2)
     [slice_3] = column_slices(at, out_video, (3,), unread=[weight_2])
     weights = [here, weight_1, weight_2, from_on[3](slice_3)]
 
-    q_theirs = jnp.concatenate(
-        [q_other[:VID], q_text, q_other[VID:], jnp.zeros((THEIRS - VID - 2 * TXTR, WIDTH), BF16)], axis=0
-    )
+    q_theirs = jnp.concatenate([q_other, q_text, jnp.zeros((THEIRS - VID - 2 * TXTR, WIDTH), BF16)], axis=0)
     queries = [q_theirs, q_video]
-    states = attend(queries, [own, r1, l1, y0], unread=weights[1:2])
+    states = attend(queries, [own, r1, l1, y0])
     states = attend(queries, [r2, l2, yr1, yl1], states)
-    states = attend(queries, [r3, l3, ry2, ly2], states, unread=weights[2:3])
+    states = attend(queries, [r3, l3, ry2, ly2], states, unread=[weights[2]])
     states = attend(queries, [r4, opposite], states)
     every = [ry3, ly3, own, r1, l1, y0, r2, l2, yr1, yl1, r3, l3, ry2, ly2, r4, opposite]
-    *theirs, sent = attend(queries[:1], [ry3, ly3], states[:2], every=every, unread=weights[3:], send=True)
+    *theirs, sent = attend(queries[:1], [ry3, ly3], states[:2], every=every, unread=[weights[3]], send=True)
     got = other_core(sent)
     mine = attend(queries[1:], [ry3, ly3], states[2:], every=every)
 

time: 291 us -> 285 us (0.979)
  transfers between devices with their start and end apart: 32 -> 32, of which waited for: 8 -> 9; matrix products, arithmetic and copies ran while one was open for 2% -> 1% of each run, Pallas kernels for 57% -> 58%
where the time goes in v2:
time: 285 us; the launch traced here: 279 us
  Pallas kernels  184 us (65%)
  starting transfers between devices  53.2 us (19%)
  waiting for transfers between devices  36.6 us (13%)
    pallas_call x6, Pallas kernels, attend(): pl.pallas_call(functools.partial(attend_kernel, groups, n, texts, first,...  173 us
    ppermute x15, waiting for transfers between devices, over_head(): return lambda value: lax.ppermute(value, 'head', pairs)  32.4 us
    ppermute x17, starting transfers between devices, over_seq(): return lambda value: lax.ppermute(value, 'seq', pairs)  30.9 us
    ppermute x15, starting transfers between devices, over_head(): return lambda value: lax.ppermute(value, 'head', pairs)  22.3 us
  transfers between devices with their start and end apart: 32, of which 9 were waited for; matrix products, arithmetic and copies ran while one was open for 1% of the time, Pallas kernels for 58%

profile of v2, /device:TPU:8, one launch (start us, length us, event | category | flops | bytes accessed | tf_op | source)
XLA Modules:
  0.0 279.4 jit_solution(8284575793188436120)
XLA Ops:
  5.2 4.0 %collective-permute-start.4 = (bf16[272,768]{1,0:T(8,128)(2,1)S(1)}, bf16[272,768]{1,0:T(8,128)(2,1)S(1)}, u32[]{:S(2)}, u32[]{:S(2)}) collective-permute-start(bf16[272,768]{1,0:T(8,128)(2,1)S(1)} %maximum_maximum_fusion.1.refs_2_.refs_3_), channel_id=1, source_target_pairs={{0,112},{8,120},{16,0},{24,8},{32,16},{40,24},{48,32},{56,40},{64,... | collective-permute-start | bytes 1253384 | tf_op jit(solution)/shard_map/ppermute | solution.py:374
  11.7 2.8 %collective-permute-start.16 = (bf16[384,768]{1,0:T(8,128)(2,1)S(1)}, bf16[384,768]{1,0:T(8,128)(2,1)S(1)}, u32[]{:S(2)}, u32[]{:S(2)}) collective-permute-start(bf16[384,768]{1,0:T(8,128)(2,1)S(1)} %get-tuple-element.42), channel_id=1, source_target_pairs={{0,6},{1,7},{2,0},{3,1},{4,2},{5,3},{6,4},{7,5},{8,14},{9,15},{10,... | collective-permute-start | bytes 1769480 | tf_op jit(solution)/shard_map/ppermute | solution.py:382
  14.5 2.3 collective-permute-start.8
  18.8 3.7 %collective-permute-start.10 = (bf16[272,768]{1,0:T(8,128)(2,1)S(1)}, bf16[272,768]{1,0:T(8,128)(2,1)S(1)}, u32[]{:S(2)}, u32[]{:S(2)}) collective-permute-start(bf16[272,768]{1,0:T(8,128)(2,1)S(1)} %collective-permute-done.4.refs_4_.refs_5_), channel_id=1, source_target_pairs={{0,112},{8,120},{16,0},{24,8},{32,16},{40,24},{48,32},{56,40},{64,... | collective-permute-start | bytes 1253384 | tf_op jit(solution)/shard_map/ppermute | solution.py:374
  22.5 2.3 collective-permute-start.5
  26.2 2.3 collective-permute-done.8.refs_0_.refs_5_.refs_6_
  31.1 36.0 %attend.6 = (f32[3,144,1024]{2,1,0:T(8,128)S(1)}, f32[3,8,1024]{2,1,0:T(8,128)S(1)}, f32[3,144,896]{2,1,0:T(8,128)S(1)}, f32[3,8,896]{2,1,0:T(8,128)S(1)}) custom-call(bf16[1024,384]{1,0:T(8,128)(2,1)S(1)} %maximum_maximum_fusion.refs_0_, bf16[896,384]{1,0:T(8,128)(2,1)S(1)} %copy-done.2, bf16[272,768]{1,0:T(8,128)(2,1)S(1)} %maximum_maximum_fusion.1.refs_2_.refs_3_, ...), custom_call_target="tpu_custom_call" | custom-call | flops 6039797760 | bytes 3317760 | tf_op jit(solution)/shard_map/attend/pallas_call | solution.py:165
  67.2 3.2 %collective-permute-start.12 = (bf16[272,768]{1,0:T(8,128)(2,1)S(1)}, bf16[272,768]{1,0:T(8,128)(2,1)S(1)}, u32[]{:S(2)}, u32[]{:S(2)}) collective-permute-start(bf16[272,768]{1,0:T(8,128)(2,1)S(1)} %collective-permute-done.10.refs_3_.refs_8_), channel_id=1, source_target_pairs={{0,112},{8,120},{16,0},{24,8},{32,16},{40,24},{48,32},{56,40},{64,... | collective-permute-start | bytes 1253384 | tf_op jit(solution)/shard_map/ppermute | solution.py:374
  70.5 3.6 %collective-permute-start.6 = (bf16[272,768]{1,0:T(8,128)(2,1)S(1)}, bf16[272,768]{1,0:T(8,128)(2,1)S(1)}, u32[]{:S(2)}, u32[]{:S(2)}) collective-permute-start(bf16[272,768]{1,0:T(8,128)(2,1)S(1)} %collective-permute-done.5.refs_5_.refs_10_), channel_id=1, source_target_pairs={{0,112},{8,120},{16,0},{24,8},{32,16},{40,24},{48,32},{56,40},{64,... | collective-permute-start | bytes 1253384 | tf_op jit(solution)/shard_map/ppermute | solution.py:374
  74.1 36.0 %attend.7 = (f32[3,144,1024]{2,1,0:T(8,128)S(1)}, f32[3,8,1024]{2,1,0:T(8,128)S(1)}, f32[3,144,896]{2,1,0:T(8,128)S(1)}, f32[3,8,896]{2,1,0:T(8,128)S(1)}) custom-call(bf16[1024,384]{1,0:T(8,128)(2,1)S(1)} %maximum_maximum_fusion.refs_0_, bf16[896,384]{1,0:T(8,128)(2,1)S(1)} %copy-done.2, ...), custom_call_target="tpu_custom_call", output_to_operand_aliasing={{0}: (6, {}), {1}: (7, {}), {2}: (8, {}), {3}: (9, {})} | custom-call | flops 6039797760 | bytes 3317760 | tf_op jit(solution)/shard_map/attend/pallas_call | solution.py:165
  110.2 4.9 %collective-permute-start.14 = (bf16[272,768]{1,0:T(8,128)(2,1)S(1)}, bf16[272,768]{1,0:T(8,128)(2,1)S(1)}, u32[]{:S(2)}, u32[]{:S(2)}) collective-permute-start(bf16[272,768]{1,0:T(8,128)(2,1)S(1)} %collective-permute-done.12.refs_3_.refs_12_), channel_id=1, source_target_pairs={{0,240},{8,248},{16,128},{24,136},{32,144},{40,152},{48,160},{56,1... | collective-permute-start | bytes 1253384 | tf_op jit(solution)/shard_map/ppermute | solution.py:374
  115.1 3.2 %collective-permute-start.7 = (bf16[272,768]{1,0:T(8,128)(2,1)S(1)}, bf16[272,768]{1,0:T(8,128)(2,1)S(1)}, u32[]{:S(2)}, u32[]{:S(2)}) collective-permute-start(bf16[272,768]{1,0:T(8,128)(2,1)S(1)} %collective-permute-done.6.refs_5_.refs_14_), channel_id=1, source_target_pairs={{0,112},{8,120},{16,0},{24,8},{32,16},{40,24},{48,32},{56,40},{64,... | collective-permute-start | bytes 1253384 | tf_op jit(solution)/shard_map/ppermute | solution.py:374
  121.1 36.0 %attend.8 = (f32[3,144,1024]{2,1,0:T(8,128)S(1)}, f32[3,8,1024]{2,1,0:T(8,128)S(1)}, f32[3,144,896]{2,1,0:T(8,128)S(1)}, f32[3,8,896]{2,1,0:T(8,128)S(1)}) custom-call(bf16[1024,384]{1,0:T(8,128)(2,1)S(1)} %maximum_maximum_fusion.refs_0_, bf16[896,384]{1,0:T(8,128)(2,1)S(1)} %copy-done.2, ...), custom_call_target="tpu_custom_call", output_to_operand_aliasing={{0}: (7, {}), {1}: (8, {}), {2}: (9, {}), {3}: (10, {})} | custom-call | flops 6039797760 | bytes 3317760 | tf_op jit(solution)/shard_map/attend/pallas_call | solution.py:165
  157.1 30.8 %attend.9 = (f32[3,144,1024]{2,1,0:T(8,128)S(1)}, f32[3,8,1024]{2,1,0:T(8,128)S(1)}, f32[3,144,896]{2,1,0:T(8,128)S(1)}, f32[3,8,896]{2,1,0:T(8,128)S(1)}) custom-call(bf16[1024,384]{1,0:T(8,128)(2,1)S(1)} %maximum_maximum_fusion.refs_0_, bf16[896,384]{1,0:T(8,128)(2,1)S(1)} %copy-done.2, ...), custom_call_target="tpu_custom_call", output_to_operand_aliasing={{0}: (4, {}), {1}: (5, {}), {2}: (6, {}), {3}: (7, {})} | custom-call | flops 3019898880 | bytes 3317760 | tf_op jit(solution)/shard_map/attend/pallas_call | solution.py:165
  187.9 18.0 %attend.11 = (f32[3,144,1024]{2,1,0:T(8,128)S(1)}, f32[3,8,1024]{2,1,0:T(8,128)S(1)}, bf16[3,144,1024]{2,1,0:T(8,128)(2,1)S(1)}) custom-call(bf16[1024,384]{1,0:T(8,128)(2,1)S(1)} %maximum_maximum_fusion.refs_0_, bf16[272,768]{1,0:T(8,128)(2,1)S(1)} %collective-permute-done.3.refs_1_, ...), custom_call_target="tpu_custom_call", output_to_operand_aliasing={{0}: (18, {}), {1}: (19, {})} | custom-call | flops 2013265920 | bytes 1769472 | tf_op jit(solution)/shard_map/attend/pallas_call | solution.py:165
  206.0 15.8 %attend.10 = (f32[3,144,896]{2,1,0:T(8,128)S(1)}, f32[3,8,896]{2,1,0:T(8,128)S(1)}) custom-call(bf16[896,384]{1,0:T(8,128)(2,1)S(1)} %copy-done.2, bf16[272,768]{1,0:T(8,128)(2,1)S(1)} %collective-permute-done.3.refs_1_, bf16[272,768]{1,0:T(8,128)(2,1)S(1)} %collective-permute-done.7.refs_2_, ...), custom_call_target="tpu_custom_call", output_to_operand_aliasing={{0}: (17, {}), {1}: (18, {})} | custom-call | flops 1761607680 | bytes 1548288 | tf_op jit(solution)/shard_map/attend/pallas_call | solution.py:165
  225.2 8.8 %collective-permute-done.20.arrived_ref.one_ref = bf16[480,384]{1,0:T(8,128)(2,1)S(1)} collective-permute-done((bf16[480,384]{1,0:T(8,128)(2,1)S(1)}, bf16[480,384]{1,0:T(8,128)(2,1)S(1)}, u32[]{:S(2)}, u32[]{:S(2)}) %collective-permute-start.20) | collective-permute-done | bytes 368672 | tf_op jit(solution)/shard_map/ppermute | solution.py:382
  234.0 2.6 collective-permute-start.22
  239.9 5.1 %collective-permute-done.21.two_ref = bf16[480,384]{1,0:T(8,128)(2,1)S(1)} collective-permute-done((bf16[480,384]{1,0:T(8,128)(2,1)S(1)}, bf16[480,384]{1,0:T(8,128)(2,1)S(1)}, u32[]{:S(2)}, u32[]{:S(2)}) %collective-permute-start.21) | collective-permute-done | bytes 368672 | tf_op jit(solution)/shard_map/ppermute | solution.py:382
  248.8 3.5 %collective-permute-done.24.one_ref.refs_2_ = bf16[480,384]{1,0:T(8,128)(2,1)S(1)} collective-permute-done((bf16[480,384]{1,0:T(8,128)(2,1)S(1)}, bf16[480,384]{1,0:T(8,128)(2,1)S(1)}, u32[]{:S(2)}, u32[]{:S(2)}) %collective-permute-start.24) | collective-permute-done | bytes 368672 | tf_op jit(solution)/shard_map/ppermute | solution.py:382
  255.9 7.8 %collective-permute-done.27.got_b = bf16[432,384]{1,0:T(8,128)(2,1)S(1)} collective-permute-done((bf16[432,384]{1,0:T(8,128)(2,1)S(1)}, bf16[432,384]{1,0:T(8,128)(2,1)S(1)}, u32[]{:S(2)}, u32[]{:S(2)}) %collective-permute-start.27) | collective-permute-done | bytes 331808 | tf_op jit(solution)/shard_map/ppermute | solution.py:382
  266.3 2.6 collective-permute-done.28
  268.8 3.1 %collective-permute-start.29 = (f32[8,1024]{1,0:T(8,128)S(1)}, f32[8,1024]{1,0:T(8,128)S(1)}, u32[]{:S(2)}, u32[]{:S(2)}) collective-permute-start(f32[8,1024]{1,0:T(8,128)S(1)} %add.9.s0_ref), channel_id=1, source_target_pairs={{0,6},{1,7},{2,0},{3,1},{4,2},{5,3},{6,4},{7,5},{8,14},{9,15},{10,... | collective-permute-start | bytes 98312 | tf_op jit(solution)/shard_map/ppermute | solution.py:382
  273.5 3.9 %collective-permute-done.30.s2_ref = f32[8,1024]{1,0:T(8,128)S(1)} collective-permute-done((f32[8,1024]{1,0:T(8,128)S(1)}, f32[8,1024]{1,0:T(8,128)S(1)}, u32[]{:S(2)}, u32[]{:S(2)}) %collective-permute-start.30) | collective-permute-done | bytes 32800 | tf_op jit(solution)/shard_map/ppermute | solution.py:382
  (84 shorter events, 35.6 us)
Async XLA Ops:
  3.2 21.6 %collective-permute-start = (bf16[272,768]{1,0:T(8,128)(2,1)S(1)}, bf16[272,768]{1,0:T(8,128)(2,1)S(1)}, u32[]{:S(2)}, u32[]{:S(2)}) collective-permute-start(bf16[272,768]{1,0:T(8,128)(2,1)S(1)} %maximum_maximum_fusion.1.refs_2_.refs_3_), channel_id=1, source_target_pairs={{0,16},{8,24},{16,32},{24,40},{32,48},{40,56},{48,64},{56,72},{64,... | collective-permute-start | bytes 1253384 | tf_op jit(solution)/shard_map/ppermute | solution.py:374
  5.2 13.6 %collective-permute-start.4 = (bf16[272,768]{1,0:T(8,128)(2,1)S(1)}, bf16[272,768]{1,0:T(8,128)(2,1)S(1)}, u32[]{:S(2)}, u32[]{:S(2)}) collective-permute-start(bf16[272,768]{1,0:T(8,128)(2,1)S(1)} %maximum_maximum_fusion.1.refs_2_.refs_3_), channel_id=1, source_target_pairs={{0,112},{8,120},{16,0},{24,8},{32,16},{40,24},{48,32},{56,40},{64,... | collective-permute-start | bytes 1253384 | tf_op jit(solution)/shard_map/ppermute | solution.py:374
  11.7 16.9 %collective-permute-start.16 = (bf16[384,768]{1,0:T(8,128)(2,1)S(1)}, bf16[384,768]{1,0:T(8,128)(2,1)S(1)}, u32[]{:S(2)}, u32[]{:S(2)}) collective-permute-start(bf16[384,768]{1,0:T(8,128)(2,1)S(1)} %get-tuple-element.42), channel_id=1, source_target_pairs={{0,6},{1,7},{2,0},{3,1},{4,2},{5,3},{6,4},{7,5},{8,14},{9,15},{10,... | collective-permute-start | bytes 1769480 | tf_op jit(solution)/shard_map/ppermute | solution.py:382
  14.5 14.0 %collective-permute-start.8 = (bf16[272,768]{1,0:T(8,128)(2,1)S(1)}, bf16[272,768]{1,0:T(8,128)(2,1)S(1)}, u32[]{:S(2)}, u32[]{:S(2)}) collective-permute-start(bf16[272,768]{1,0:T(8,128)(2,1)S(1)} %maximum_maximum_fusion.1.refs_2_.refs_3_), channel_id=1, source_target_pairs={{0,128},{8,136},{16,144},{24,152},{32,160},{40,168},{48,176},{56,1... | collective-permute-start | bytes 1253384 | tf_op jit(solution)/shard_map/ppermute | solution.py:374
  18.8 48.4 %collective-permute-start.10 = (bf16[272,768]{1,0:T(8,128)(2,1)S(1)}, bf16[272,768]{1,0:T(8,128)(2,1)S(1)}, u32[]{:S(2)}, u32[]{:S(2)}) collective-permute-start(bf16[272,768]{1,0:T(8,128)(2,1)S(1)} %collective-permute-done.4.refs_4_.refs_5_), channel_id=1, source_target_pairs={{0,112},{8,120},{16,0},{24,8},{32,16},{40,24},{48,32},{56,40},{64,... | collective-permute-start | bytes 1253384 | tf_op jit(solution)/shard_map/ppermute | solution.py:374
  22.5 48.0 %collective-permute-start.5 = (bf16[272,768]{1,0:T(8,128)(2,1)S(1)}, bf16[272,768]{1,0:T(8,128)(2,1)S(1)}, u32[]{:S(2)}, u32[]{:S(2)}) collective-permute-start(bf16[272,768]{1,0:T(8,128)(2,1)S(1)} %collective-permute-done.4.refs_4_.refs_5_), channel_id=1, source_target_pairs={{0,128},{8,136},{16,144},{24,152},{32,160},{40,168},{48,176},{56,1... | collective-permute-start | bytes 1253384 | tf_op jit(solution)/shard_map/ppermute | solution.py:374
  24.8 45.6 %collective-permute-start.1 = (bf16[272,768]{1,0:T(8,128)(2,1)S(1)}, bf16[272,768]{1,0:T(8,128)(2,1)S(1)}, u32[]{:S(2)}, u32[]{:S(2)}) collective-permute-start(bf16[272,768]{1,0:T(8,128)(2,1)S(1)} %collective-permute-done.refs_3_.refs_4_), channel_id=1, source_target_pairs={{0,128},{8,136},{16,144},{24,152},{32,160},{40,168},{48,176},{56,1... | collective-permute-start | bytes 1253384 | tf_op jit(solution)/shard_map/ppermute | solution.py:374
  28.5 38.6 %collective-permute-start.9 = (bf16[272,768]{1,0:T(8,128)(2,1)S(1)}, bf16[272,768]{1,0:T(8,128)(2,1)S(1)}, u32[]{:S(2)}, u32[]{:S(2)}) collective-permute-start(bf16[272,768]{1,0:T(8,128)(2,1)S(1)} %collective-permute-done.refs_3_.refs_4_), channel_id=1, source_target_pairs={{0,16},{8,24},{16,32},{24,40},{32,48},{40,56},{48,64},{56,72},{64,... | collective-permute-start | bytes 1253384 | tf_op jit(solution)/shard_map/ppermute | solution.py:374
  29.2 89.2 %collective-permute-start.17 = (bf16[384,768]{1,0:T(8,128)(2,1)S(1)}, bf16[384,768]{1,0:T(8,128)(2,1)S(1)}, u32[]{:S(2)}, u32[]{:S(2)}) collective-permute-start(bf16[384,768]{1,0:T(8,128)(2,1)S(1)} %columns.4), channel_id=1, source_target_pairs={{0,4},{1,5},{2,6},{3,7},{4,0},{5,1},{6,2},{7,3},{8,12},{9,13},{10,... | collective-permute-start | bytes 1769480 | tf_op jit(solution)/shard_map/ppermute | solution.py:382
  67.1 42.9 %collective-permute-start.11 = (bf16[272,768]{1,0:T(8,128)(2,1)S(1)}, bf16[272,768]{1,0:T(8,128)(2,1)S(1)}, u32[]{:S(2)}, u32[]{:S(2)}) collective-permute-start(bf16[272,768]{1,0:T(8,128)(2,1)S(1)} %collective-permute-done.9.refs_2_.refs_7_), channel_id=1, source_target_pairs={{0,16},{8,24},{16,32},{24,40},{32,48},{40,56},{48,64},{56,72},{64,... | collective-permute-start | bytes 1253384 | tf_op jit(solution)/shard_map/ppermute | solution.py:374
  67.2 42.9 %collective-permute-start.12 = (bf16[272,768]{1,0:T(8,128)(2,1)S(1)}, bf16[272,768]{1,0:T(8,128)(2,1)S(1)}, u32[]{:S(2)}, u32[]{:S(2)}) collective-permute-start(bf16[272,768]{1,0:T(8,128)(2,1)S(1)} %collective-permute-done.10.refs_3_.refs_8_), channel_id=1, source_target_pairs={{0,112},{8,120},{16,0},{24,8},{32,16},{40,24},{48,32},{56,40},{64,... | collective-permute-start | bytes 1253384 | tf_op jit(solution)/shard_map/ppermute | solution.py:374
  70.5 44.7 %collective-permute-start.2 = (bf16[272,768]{1,0:T(8,128)(2,1)S(1)}, bf16[272,768]{1,0:T(8,128)(2,1)S(1)}, u32[]{:S(2)}, u32[]{:S(2)}) collective-permute-start(bf16[272,768]{1,0:T(8,128)(2,1)S(1)} %collective-permute-done.1.refs_4_.refs_9_), channel_id=1, source_target_pairs={{0,16},{8,24},{16,32},{24,40},{32,48},{40,56},{48,64},{56,72},{64,... | collective-permute-start | bytes 1253384 | tf_op jit(solution)/shard_map/ppermute | solution.py:374
  70.5 44.7 %collective-permute-start.6 = (bf16[272,768]{1,0:T(8,128)(2,1)S(1)}, bf16[272,768]{1,0:T(8,128)(2,1)S(1)}, u32[]{:S(2)}, u32[]{:S(2)}) collective-permute-start(bf16[272,768]{1,0:T(8,128)(2,1)S(1)} %collective-permute-done.5.refs_5_.refs_10_), channel_id=1, source_target_pairs={{0,112},{8,120},{16,0},{24,8},{32,16},{40,24},{48,32},{56,40},{64,... | collective-permute-start | bytes 1253384 | tf_op jit(solution)/shard_map/ppermute | solution.py:374
  110.1 47.0 %collective-permute-start.13 = (bf16[272,768]{1,0:T(8,128)(2,1)S(1)}, bf16[272,768]{1,0:T(8,128)(2,1)S(1)}, u32[]{:S(2)}, u32[]{:S(2)}) collective-permute-start(bf16[272,768]{1,0:T(8,128)(2,1)S(1)} %collective-permute-done.11.refs_2_.refs_11_), channel_id=1, source_target_pairs={{0,16},{8,24},{16,32},{24,40},{32,48},{40,56},{48,64},{56,72},{64,... | collective-permute-start | bytes 1253384 | tf_op jit(solution)/shard_map/ppermute | solution.py:374
  110.2 46.9 %collective-permute-start.14 = (bf16[272,768]{1,0:T(8,128)(2,1)S(1)}, bf16[272,768]{1,0:T(8,128)(2,1)S(1)}, u32[]{:S(2)}, u32[]{:S(2)}) collective-permute-start(bf16[272,768]{1,0:T(8,128)(2,1)S(1)} %collective-permute-done.12.refs_3_.refs_12_), channel_id=1, source_target_pairs={{0,240},{8,248},{16,128},{24,136},{32,144},{40,152},{48,160},{56,1... | collective-permute-start | bytes 1253384 | tf_op jit(solution)/shard_map/ppermute | solution.py:374
  115.1 72.7 %collective-permute-start.3 = (bf16[272,768]{1,0:T(8,128)(2,1)S(1)}, bf16[272,768]{1,0:T(8,128)(2,1)S(1)}, u32[]{:S(2)}, u32[]{:S(2)}) collective-permute-start(bf16[272,768]{1,0:T(8,128)(2,1)S(1)} %collective-permute-done.2.refs_4_.refs_13_), channel_id=1, source_target_pairs={{0,16},{8,24},{16,32},{24,40},{32,48},{40,56},{48,64},{56,72},{64,... | collective-permute-start | bytes 1253384 | tf_op jit(solution)/shard_map/ppermute | solution.py:374
  115.1 72.7 %collective-permute-start.7 = (bf16[272,768]{1,0:T(8,128)(2,1)S(1)}, bf16[272,768]{1,0:T(8,128)(2,1)S(1)}, u32[]{:S(2)}, u32[]{:S(2)}) collective-permute-start(bf16[272,768]{1,0:T(8,128)(2,1)S(1)} %collective-permute-done.6.refs_5_.refs_14_), channel_id=1, source_target_pairs={{0,112},{8,120},{16,0},{24,8},{32,16},{40,24},{48,32},{56,40},{64,... | collective-permute-start | bytes 1253384 | tf_op jit(solution)/shard_map/ppermute | solution.py:374
  119.0 68.9 %collective-permute-start.18 = (bf16[384,768]{1,0:T(8,128)(2,1)S(1)}, bf16[384,768]{1,0:T(8,128)(2,1)S(1)}, u32[]{:S(2)}, u32[]{:S(2)}) collective-permute-start(bf16[384,768]{1,0:T(8,128)(2,1)S(1)} %columns.5), channel_id=1, source_target_pairs={{0,2},{1,3},{2,4},{3,5},{4,6},{5,7},{6,0},{7,1},{8,10},{9,11},{10,... | collective-permute-start | bytes 1769480 | tf_op jit(solution)/shard_map/ppermute | solution.py:382
  205.9 15.9 %collective-permute-start.19 = (bf16[3,144,1024]{2,1,0:T(8,128)(2,1)S(1)}, bf16[3,144,1024]{2,1,0:T(8,128)(2,1)S(1)}, u32[]{:S(2)}, u32[]{:S(2)}) collective-permute-start(bf16[3,144,1024]{2,1,0:T(8,128)(2,1)S(1)} %get-tuple-element.63), channel_id=1, source_target_pairs={{0,8},{8,0},{16,24},{24,16},{32,40},{40,32},{48,56},{56,48},{64,72... | collective-permute-start | bytes 2654216 | tf_op jit(solution)/shard_map/ppermute | solution.py:374
  224.5 13.2 %collective-permute-start.25 = (bf16[480,384]{1,0:T(8,128)(2,1)S(1)}, bf16[480,384]{1,0:T(8,128)(2,1)S(1)}, u32[]{:S(2)}, u32[]{:S(2)}) collective-permute-start(bf16[480,384]{1,0:T(8,128)(2,1)S(1)} %get-tuple-element.65.lower_ref.refs_1_), channel_id=1, source_target_pairs={{0,2},{1,3},{2,4},{3,5},{4,6},{5,7},{6,0},{7,1},{8,10},{9,11},{10,... | collective-permute-start | bytes 1105928 | tf_op jit(solution)/shard_map/ppermute | solution.py:382
  225.1 20.0 %collective-permute-start.21 = (bf16[480,384]{1,0:T(8,128)(2,1)S(1)}, bf16[480,384]{1,0:T(8,128)(2,1)S(1)}, u32[]{:S(2)}, u32[]{:S(2)}) collective-permute-start(bf16[480,384]{1,0:T(8,128)(2,1)S(1)} %get-tuple-element.64.upper_ref), channel_id=1, source_target_pairs={{0,2},{1,3},{2,4},{3,5},{4,6},{5,7},{6,0},{7,1},{8,10},{9,11},{10,... | collective-permute-start | bytes 1105928 | tf_op jit(solution)/shard_map/ppermute | solution.py:382
  237.6 14.7 %collective-permute-start.24 = (bf16[480,384]{1,0:T(8,128)(2,1)S(1)}, bf16[480,384]{1,0:T(8,128)(2,1)S(1)}, u32[]{:S(2)}, u32[]{:S(2)}) collective-permute-start(bf16[480,384]{1,0:T(8,128)(2,1)S(1)} %get-tuple-element.71), channel_id=1, source_target_pairs={{0,6},{1,7},{2,0},{3,1},{4,2},{5,3},{6,4},{7,5},{8,14},{9,15},{10,... | collective-permute-start | bytes 1105928 | tf_op jit(solution)/shard_map/ppermute | solution.py:382
  237.7 15.7 %collective-permute-start.26 = (bf16[480,384]{1,0:T(8,128)(2,1)S(1)}, bf16[480,384]{1,0:T(8,128)(2,1)S(1)}, u32[]{:S(2)}, u32[]{:S(2)}) collective-permute-start(bf16[480,384]{1,0:T(8,128)(2,1)S(1)} %collective-permute-done.25.two_ref.refs_3_), channel_id=1, source_target_pairs={{0,2},{1,3},{2,4},{3,5},{4,6},{5,7},{6,0},{7,1},{8,10},{9,11},{10,... | collective-permute-start | bytes 1105928 | tf_op jit(solution)/shard_map/ppermute | solution.py:382
  247.4 16.3 %collective-permute-start.23 = (bf16[480,384]{1,0:T(8,128)(2,1)S(1)}, bf16[480,384]{1,0:T(8,128)(2,1)S(1)}, u32[]{:S(2)}, u32[]{:S(2)}) collective-permute-start(bf16[480,384]{1,0:T(8,128)(2,1)S(1)} %get-tuple-element.69), channel_id=1, source_target_pairs={{0,1},{1,0},{2,3},{3,2},{4,5},{5,4},{6,7},{7,6},{8,9},{9,8},{10,11... | collective-permute-start | bytes 1105928 | tf_op jit(solution)/shard_map/ppermute | solution.py:382
  (17 other events, 184.2 us)
